TPU v7x, 32 devices: a whole 2x2x4 slice. The times are simulated.
32 devices in a mesh: dp: 4 (over z), pipe: 4 (over x, core), mp: 2 (over y).
Axes of the slice: x: 2, y: 2, z: 4, core: 2. Of those that a mesh axis runs over, the one named last changes fastest.
Arguments:
- latents: bfloat16 [4, 2, 64, 3072], P('dp'), may hold values from -6 to 6
- caption_kv: bfloat16 [4, 4, 2, 128, 1536], P('dp', 'pipe', None, None, 'mp'), may hold values from -6 to 6
- caption_mask: int32 [4, 128], P('dp'), may hold values from 0 to 1, as said below
- query_weight: bfloat16 [4, 3072, 1536], P('pipe', None, 'mp'), may hold values from -0.109375 to 0.109375
- out_weight: bfloat16 [4, 1536, 3072], P('pipe', 'mp'), may hold values from -0.15625 to 0.15625
- gate: float32 [4, 3072], P('pipe'), may hold values from 0.5 to 1.5
- cotangent: bfloat16 [4, 2, 64, 3072], P('dp'), may hold values from -6 to 6
Outputs:
- section_out: bfloat16 [4, 4, 2, 64, 3072], P('pipe', 'dp', None, None, 'mp')
- input_grad: bfloat16 [4, 4, 2, 64, 3072], P('pipe', 'dp', None, None, 'mp')
- out_weight_grad: float32 [4, 1536, 3072], P('pipe', 'mp', 'dp')
Inputs may be any that keep to these rules, and one draw needn't show every extreme that they name: `caption_mask`: each row is a run of ones followed by zeros; the first 32 entries of every row are 1, and some row is all ones.
All inputs are finite; a program needn't handle non-finite values.
Results may differ from a plain program's by a relative error of at most 0.04.
Values may be sent and summed in bfloat16 or wider, within the bound.
A program may use at most 64 MiB of HBM per device.

v0:
```python
import math

import jax
import jax.numpy as jnp
from jax import lax
from jax.sharding import PartitionSpec as P

HEAD_DIM = 128


def from_behind(value, axis, steps):
    count = lax.axis_size(axis)
    leading, last = (max(0, -steps), min(count, count - steps))
    return lax.ppermute(value, axis, [(source, source + steps) for source in range(leading, last)])


def forward_parts(x_rows, w_query, kv_pair, live):
    rows = x_rows.shape[0]
    x_float = x_rows.astype(jnp.float32)
    scale_r = lax.rsqrt(jnp.mean(x_float * x_float, axis=-1, keepdims=True) + 1e-06)
    normed = (x_float * scale_r).astype(jnp.bfloat16)
    query = jnp.dot(normed, w_query, preferred_element_type=jnp.float32).astype(jnp.bfloat16)
    q_heads = query.reshape(rows, -1, HEAD_DIM).astype(jnp.float32)
    k_heads = kv_pair[0].reshape(kv_pair.shape[1], -1, HEAD_DIM).astype(jnp.float32)
    v_heads = kv_pair[1].reshape(kv_pair.shape[1], -1, HEAD_DIM).astype(jnp.float32)
    scores = jnp.einsum("rhd,chd->hrc", q_heads, k_heads) / math.sqrt(HEAD_DIM)
    scores = jnp.where(live[None, None, :] > 0, scores, -1e30)
    prob = jax.nn.softmax(scores, axis=-1)
    probs = lax.optimization_barrier(prob.astype(jnp.bfloat16)).astype(jnp.float32)
    attended = jnp.einsum("hrc,chd->rhd", probs, v_heads).reshape(rows, -1).astype(jnp.bfloat16)
    return (x_float, scale_r, prob, attended, k_heads, v_heads)


def forward_local(x_rows, w_query, w_out, kv_pair, live):
    parts = forward_parts(x_rows, w_query, kv_pair, live)
    return jnp.dot(parts[3], w_out, preferred_element_type=jnp.float32)


def backward_local(x_rows, grad_rows, w_query, w_out, kv_pair, live, gain):
    rows = x_rows.shape[0]
    x_float, scale_r, prob, attended, k_heads, v_heads = forward_parts(
        x_rows, w_query, kv_pair, live
    )
    dproj = (gain * grad_rows.astype(jnp.float32)).astype(jnp.bfloat16)
    dattended = jnp.dot(dproj, w_out.T, preferred_element_type=jnp.float32).astype(jnp.bfloat16)
    d_heads = dattended.reshape(rows, -1, HEAD_DIM).astype(jnp.float32)
    dprob = jnp.einsum("rhd,chd->hrc", d_heads, v_heads)
    dscore = (prob * (dprob - jnp.sum(prob * dprob, axis=-1, keepdims=True))).astype(jnp.bfloat16)
    dscore_f = lax.optimization_barrier(dscore).astype(jnp.float32)
    dquery = (
        (jnp.einsum("hrc,chd->rhd", dscore_f, k_heads) / math.sqrt(HEAD_DIM))
        .reshape(rows, -1)
        .astype(jnp.bfloat16)
    )
    partial_dn = jnp.dot(dquery, w_query.T, preferred_element_type=jnp.float32)
    return (partial_dn, attended, dproj)


def per_device(latents, caption_kv, caption_mask, query_weight, out_weight, gate, cotangent):
    micro, tok, width = (latents.shape[1], latents.shape[2], latents.shape[3])
    rows = micro * tok
    w_query = query_weight[0]
    w_out = out_weight[0]
    kv_pair = caption_kv[0, 0]
    live = caption_mask[0]
    gain = gate[0]
    inner_width = w_out.shape[0]
    sections = lax.axis_size("pipe")
    position = lax.axis_index("pipe")
    share = width // lax.axis_size("mp")
    offset = lax.axis_index("mp") * share

    def own_part(values):
        return lax.dynamic_slice_in_dim(values, offset, share, 1)

    def forward_busy(x_rows):
        return forward_local(x_rows, w_query, w_out, kv_pair, live)

    def forward_quiet(x_rows):
        return jnp.zeros((rows, width), jnp.float32)

    def forward_turn(step, carry):
        current, saved, result = carry
        mine = position == step
        partial_proj = lax.cond(mine, forward_busy, forward_quiet, current)
        x_now = current.astype(jnp.float32)
        proj = lax.psum(partial_proj.astype(jnp.bfloat16), "mp").astype(jnp.float32)
        output = (x_now + gain * proj).astype(jnp.bfloat16)
        output_share = own_part(output)
        arrived = from_behind(output, "pipe", 1)
        saved = jnp.where(mine, current, saved)
        result = jnp.where(mine, output_share, result)
        current = jnp.where(position == step + 1, arrived, current)
        return (current, saved, result)

    start = latents.reshape(rows, width)
    _, saved, result = lax.fori_loop(0, sections, forward_turn, (start, start, own_part(start)))

    def backward_busy(operands):
        return backward_local(operands[0], operands[1], w_query, w_out, kv_pair, live, gain)

    def backward_quiet(operands):
        return (
            jnp.zeros((rows, width), jnp.float32),
            jnp.zeros((rows, inner_width), jnp.bfloat16),
            jnp.zeros((rows, width), jnp.bfloat16),
        )

    x_float = saved.astype(jnp.float32)
    scale_r = lax.rsqrt(jnp.mean(x_float * x_float, axis=-1, keepdims=True) + 1e-06)

    def backward_turn(count, carry):
        incoming, grad_in, attended, dproj = carry
        active = sections - 1 - count
        mine = position == active
        partial_dn, attended_now, dproj_now = lax.cond(
            mine, backward_busy, backward_quiet, (saved, incoming)
        )
        dnormed = lax.psum(partial_dn.astype(jnp.bfloat16), "mp").astype(jnp.float32)
        inner = jnp.mean(dnormed * x_float, axis=-1, keepdims=True)
        dx = (
            incoming.astype(jnp.float32)
            + scale_r * (dnormed - x_float * (scale_r * scale_r) * inner)
        ).astype(jnp.bfloat16)
        dx_share = own_part(dx)
        arrived = from_behind(dx, "pipe", -1)
        grad_in = jnp.where(mine, dx_share, grad_in)
        attended = jnp.where(mine, attended_now, attended)
        dproj = jnp.where(mine, dproj_now, dproj)
        incoming = jnp.where(position == active - 1, arrived, incoming)
        return (incoming, grad_in, attended, dproj)

    incoming0 = cotangent.reshape(rows, width)
    init = (
        incoming0,
        own_part(incoming0),
        jnp.zeros((rows, inner_width), jnp.bfloat16),
        jnp.zeros((rows, width), jnp.bfloat16),
    )
    _, grad_in, attended, dproj = lax.fori_loop(0, sections, backward_turn, init)
    columns = lax.all_to_all(dproj, "dp", split_axis=1, concat_axis=0, tiled=True)
    weight_grad = lax.dot_general(
        lax.all_gather(attended, "dp", axis=0, tiled=True),
        columns,
        (((0,), (0,)), ((), ())),
        preferred_element_type=jnp.float32,
    )
    section_out = result.reshape(1, 1, micro, tok, share)
    input_grad = grad_in.reshape(1, 1, micro, tok, share)
    return (section_out, input_grad, weight_grad[None])


def solution(mesh):
    return jax.shard_map(
        per_device,
        mesh=mesh,
        in_specs=(
            P("dp", None, None, None),
            P("dp", "pipe", None, None, "mp"),
            P("dp", None),
            P("pipe", None, "mp"),
            P("pipe", "mp", None),
            P("pipe", None),
            P("dp", None, None, None),
        ),
        out_specs=(
            P("pipe", "dp", None, None, "mp"),
            P("pipe", "dp", None, None, "mp"),
            P("pipe", "mp", "dp"),
        ),
        check_vma=False,
    )
```

profile of v0, /device:TPU:0, one launch (start us, length us, event | category | flops | bytes accessed | tf_op | source)
XLA Modules:
  0.0 590.5 jit_solution(10184305833692540957)
XLA Ops:
  10.7 228.3 %while.43 = (s32[]{:T(128)}, bf16[128,3072]{1,0:T(8,128)(2,1)S(1)}, bf16[128,3072]{1,0:T(8,128)(2,1)S(1)}, bf16[128,1536]{1,0:T(8,128)(2,1)}, s32[]{:T(128)}, /*...) while((s32[]{:T(128)}, bf16[128,3072]{1,0:T(8,128)(2,1)S(1)}, ...), condition=%wide.region_7.8_spmd, body=%wide.region_0.7_spmd.sunk | while | flops 1264779648 | bytes 33838128 | solution.py:97
  10.7 10.2 %conditional.5 = (bf16[128,3072]{1,0:T(8,128)(2,1)S(1)}) conditional(s32[]{:T(128)} %convert_element_type.249, () %tuple.111, (s32[1,128]{1,0:T(1,128)}, bf16[128,3072]{1,0:T(8,128)(2,1)S(1)}, bf16[3072,768]{1,0:T(8,128)(2,1)}, bf16[2,128,768]{1,2,0:T(8,128)(2,1)S(1)}, bf16[768,3072]{1,0:T(8,128)(2,1)}) %tuple.112), branch_computations={%region_1.0_spmd, %region_2.5_spmd} | conditional | flops 1261437312 | bytes 15344392 | solution.py:85
  10.9 3.2 convolution_convert_fusion.1
  16.2 1.3 fusion.29
  17.7 3.2 fusion.34
  21.8 36.3 %all-reduce.3.cloned.1.call-done = bf16[128,3072]{1,0:T(8,128)(2,1)} async-done(((bf16[128,3072]{1,0:T(8,128)(2,1)}), bf16[128,3072]{1,0:T(8,128)(2,1)}) %all-reduce.3.cloned.1.call-update) | async-done | bytes 786448 | tf_op jit(solution)/shard_map/while/body/eval_jaxpr/psum | solution.py:87
  58.1 1.4 add_convert_fusion.2
  59.4 2.6 collective-permute-start
  64.7 53.1 %all-reduce.3.cloned.1.call-done = bf16[128,3072]{1,0:T(8,128)(2,1)} async-done(((bf16[128,3072]{1,0:T(8,128)(2,1)}), bf16[128,3072]{1,0:T(8,128)(2,1)}) %all-reduce.3.cloned.1.call-update) | async-done | bytes 786448 | tf_op jit(solution)/shard_map/while/body/eval_jaxpr/psum | solution.py:87
  117.8 1.4 add_convert_fusion.2
  119.2 2.6 collective-permute-start
  121.8 1.8 dynamic-slice_select_fusion.4
  125.1 54.7 %all-reduce.3.cloned.1.call-done = bf16[128,3072]{1,0:T(8,128)(2,1)} async-done(((bf16[128,3072]{1,0:T(8,128)(2,1)}), bf16[128,3072]{1,0:T(8,128)(2,1)}) %all-reduce.3.cloned.1.call-update) | async-done | bytes 786448 | tf_op jit(solution)/shard_map/while/body/eval_jaxpr/psum | solution.py:87
  179.8 1.4 add_convert_fusion.2
  181.2 2.6 collective-permute-start
  183.8 1.8 dynamic-slice_select_fusion.4
  187.1 45.6 %all-reduce.3.cloned.1.call-done = bf16[128,3072]{1,0:T(8,128)(2,1)} async-done(((bf16[128,3072]{1,0:T(8,128)(2,1)}), bf16[128,3072]{1,0:T(8,128)(2,1)}) %all-reduce.3.cloned.1.call-update) | async-done | bytes 786448 | tf_op jit(solution)/shard_map/while/body/eval_jaxpr/psum | solution.py:87
  232.8 1.4 add_convert_fusion.2
  234.1 2.6 collective-permute-start
  236.8 1.8 dynamic-slice_select_fusion.4
  240.6 302.5 %while.44 = (s32[]{:T(128)}, bf16[128,3072]{1,0:T(8,128)(2,1)S(1)}, bf16[128,1536]{1,0:T(8,128)(2,1)}, bf16[128,768]{0,1:T(8,128)(2,1)}, bf16[128,3072]{1,0:T(8,...) while((s32[]{:T(128)}, bf16[128,3072]{1,0:T(8,128)(2,1)S(1)}, ...), condition=%wide.region_18.19_spmd.clone, body=%wide.region_9.18_spmd.clone.sunk | while | flops 1949271296 | bytes 50754816 | solution.py:140
  240.7 2.7 conditional.6
  243.4 58.5 %all-reduce.5.cloned.1.call-done = bf16[128,3072]{1,0:T(8,128)(2,1)} async-done(((bf16[128,3072]{1,0:T(8,128)(2,1)}), bf16[128,3072]{1,0:T(8,128)(2,1)}) %all-reduce.5.cloned.1.call-update) | async-done | bytes 786448 | tf_op jit(solution)/shard_map/while/body/eval_jaxpr/psum | solution.py:119
  301.9 1.4 fusion.62
  303.3 2.1 fusion.63
  305.5 1.3 collective-permute-start.1
  308.4 2.0 dynamic-slice_select_fusion.5
  310.7 2.7 conditional.6
  313.4 66.9 %all-reduce.5.cloned.1.call-done = bf16[128,3072]{1,0:T(8,128)(2,1)} async-done(((bf16[128,3072]{1,0:T(8,128)(2,1)}), bf16[128,3072]{1,0:T(8,128)(2,1)}) %all-reduce.5.cloned.1.call-update) | async-done | bytes 786448 | tf_op jit(solution)/shard_map/while/body/eval_jaxpr/psum | solution.py:119
  380.3 1.4 fusion.62
  381.8 2.1 fusion.63
  383.9 1.3 collective-permute-start.1
  385.2 2.1 select_select_fusion.5
  387.3 1.6 select_select_fusion.4
  388.9 2.0 dynamic-slice_select_fusion.5
  391.2 2.7 conditional.6
  393.9 65.4 %all-reduce.5.cloned.1.call-done = bf16[128,3072]{1,0:T(8,128)(2,1)} async-done(((bf16[128,3072]{1,0:T(8,128)(2,1)}), bf16[128,3072]{1,0:T(8,128)(2,1)}) %all-reduce.5.cloned.1.call-update) | async-done | bytes 786448 | tf_op jit(solution)/shard_map/while/body/eval_jaxpr/psum | solution.py:119
  459.3 1.4 fusion.62
  460.7 2.1 fusion.63
  462.9 1.3 collective-permute-start.1
  464.2 2.1 select_select_fusion.5
  466.3 1.6 select_select_fusion.4
  467.9 2.0 dynamic-slice_select_fusion.5
  469.8 1.3 broadcast_select_fusion.6
  471.3 27.2 %conditional.6 = (bf16[128,3072]{1,0:T(8,128)(2,1)}, bf16[128,768]{0,1:T(8,128)(2,1)}, bf16[128,3072]{1,0:T(8,128)(2,1)}) conditional(s32[]{:T(128)} %convert_element_type.254, () %tuple.114, (s32[1,128]{1,0:T(1,128)}, bf16[128,3072]{1,0:T(8,128)(2,1)S(1)}, bf16[3072,768]{1,0:T(8,128)(2,1)}, bf16[2,128,768]{1,2,0:T(8,128)(2,1)S(1)}, ...), branch_computations={%region_10.10_spmd, %region_11.15_spmd} | conditional | flops 1942979840 | bytes 26959696 | solution.py:116
  472.5 3.9 convolution_convert_fusion.4
  476.3 1.7 copy.36
  478.8 1.3 compare_bitcast_fusion.1
  480.1 2.1 fusion.31
  482.2 4.9 convolution_convert_fusion.3
  487.2 1.7 copy.39
  488.9 2.4 fusion.17
  492.5 5.0 fusion.35
  498.5 33.6 %all-reduce.5.cloned.1.call-done = bf16[128,3072]{1,0:T(8,128)(2,1)} async-done(((bf16[128,3072]{1,0:T(8,128)(2,1)}), bf16[128,3072]{1,0:T(8,128)(2,1)}) %all-reduce.5.cloned.1.call-update) | async-done | bytes 786448 | tf_op jit(solution)/shard_map/while/body/eval_jaxpr/psum | solution.py:119
  532.1 1.4 fusion.62
  533.6 2.1 fusion.63
  535.7 1.3 collective-permute-start.1
  537.0 2.3 select_select_fusion.5
  539.3 1.7 select_select_fusion.4
  541.0 1.8 dynamic-slice_select_fusion.5
  543.1 2.3 copy.45
  545.4 4.6 all-to-all-start
  550.0 31.2 %all_gather.3 = bf16[512,768]{0,1:T(8,128)(2,1)S(1)} all-gather(bf16[128,768]{0,1:T(8,128)(2,1)S(1)} %copy-done.4), channel_id=1, replica_groups=mesh['dp'=4,'pipe'=4,'mp'=2] {'dp'}, dimensions={0}, use_global_device_ids=true | all-gather | bytes 983040 | tf_op jit(solution)/shard_map/all_gather | solution.py:143
  581.5 2.2 convolution_bitcast_fusion
  (115 shorter events, 29.5 us)
Async XLA Ops:
  7.2 1.4 copy-start.6
  8.5 1.0 copy-start.7
  8.7 2.0 copy-start.5
  10.7 47.4 %all-reduce.3.cloned.1.call-start = ((), (), s32[]{:S(2)}) async-start(), calls=%async_computation.1 | async-start | bytes 1572864 | tf_op jit(solution)/shard_map/while/body/eval_jaxpr/psum | solution.py:87
  20.9 0.9 copy-start.1
  59.4 3.8 collective-permute-start
  63.6 54.2 %all-reduce.3.cloned.1.call-start = ((), (), s32[]{:S(2)}) async-start(), calls=%async_computation.1 | async-start | bytes 1572864 | tf_op jit(solution)/shard_map/while/body/eval_jaxpr/psum | solution.py:87
  63.8 0.9 copy-start.1
  119.2 4.5 collective-permute-start
  124.1 55.7 %all-reduce.3.cloned.1.call-start = ((), (), s32[]{:S(2)}) async-start(), calls=%async_computation.1 | async-start | bytes 1572864 | tf_op jit(solution)/shard_map/while/body/eval_jaxpr/psum | solution.py:87
  124.2 0.9 copy-start.1
  181.2 4.5 collective-permute-start
  186.1 46.7 %all-reduce.3.cloned.1.call-start = ((), (), s32[]{:S(2)}) async-start(), calls=%async_computation.1 | async-start | bytes 1572864 | tf_op jit(solution)/shard_map/while/body/eval_jaxpr/psum | solution.py:87
  186.2 0.9 copy-start.1
  234.1 4.5 collective-permute-start
  240.6 61.3 %all-reduce.5.cloned.1.call-start = ((), (), s32[]{:S(2)}) async-start(), calls=%async_computation.2 | async-start | bytes 1572864 | tf_op jit(solution)/shard_map/while/body/eval_jaxpr/psum | solution.py:119
  243.3 60.0 %copy-start.8 = (f32[128,1]{0,1:T(1,128)S(1)}, f32[128,1]{0,1:T(1,128)}, u32[]{:S(2)}) copy-start(f32[128,1]{0,1:T(1,128)} %get-tuple-element.1194) | copy-start | bytes 1540 | tf_op jit(solution)/shard_map/while
  301.9 1.5 copy-start
  305.5 4.9 collective-permute-start.1
  310.6 69.7 %all-reduce.5.cloned.1.call-start = ((), (), s32[]{:S(2)}) async-start(), calls=%async_computation.2 | async-start | bytes 1572864 | tf_op jit(solution)/shard_map/while/body/eval_jaxpr/psum | solution.py:119
  313.4 68.4 %copy-start.8 = (f32[128,1]{0,1:T(1,128)S(1)}, f32[128,1]{0,1:T(1,128)}, u32[]{:S(2)}) copy-start(f32[128,1]{0,1:T(1,128)} %get-tuple-element.1194) | copy-start | bytes 1540 | tf_op jit(solution)/shard_map/while
  380.3 1.5 copy-start
  383.9 7.0 %collective-permute-start.1 = (bf16[128,3072]{1,0:T(8,128)(2,1)}, bf16[128,3072]{1,0:T(8,128)(2,1)}, u32[]{:S(2)}, u32[]{:S(2)}) collective-permute-start(bf16[128,3072]{1,0:T(8,128)(2,1)} %fusion.63), channel_id=1, source_target_pairs={{2,0},{4,2},{6,4},{3,1},{5,3},{7,5},{10,8},{12,10},{14,12},{11,9},... | collective-permute-start | bytes 2359304 | tf_op jit(solution)/shard_map/while/body/eval_jaxpr/ppermute | solution.py:14
  391.1 68.1 %all-reduce.5.cloned.1.call-start = ((), (), s32[]{:S(2)}) async-start(), calls=%async_computation.2 | async-start | bytes 1572864 | tf_op jit(solution)/shard_map/while/body/eval_jaxpr/psum | solution.py:119
  393.9 66.9 %copy-start.8 = (f32[128,1]{0,1:T(1,128)S(1)}, f32[128,1]{0,1:T(1,128)}, u32[]{:S(2)}) copy-start(f32[128,1]{0,1:T(1,128)} %get-tuple-element.1194) | copy-start | bytes 1540 | tf_op jit(solution)/shard_map/while
  459.3 1.5 copy-start
  462.9 7.0 %collective-permute-start.1 = (bf16[128,3072]{1,0:T(8,128)(2,1)}, bf16[128,3072]{1,0:T(8,128)(2,1)}, u32[]{:S(2)}, u32[]{:S(2)}) collective-permute-start(bf16[128,3072]{1,0:T(8,128)(2,1)} %fusion.63), channel_id=1, source_target_pairs={{2,0},{4,2},{6,4},{3,1},{5,3},{7,5},{10,8},{12,10},{14,12},{11,9},... | collective-permute-start | bytes 2359304 | tf_op jit(solution)/shard_map/while/body/eval_jaxpr/ppermute | solution.py:14
  471.2 60.9 %all-reduce.5.cloned.1.call-start = ((), (), s32[]{:S(2)}) async-start(), calls=%async_computation.2 | async-start | bytes 1572864 | tf_op jit(solution)/shard_map/while/body/eval_jaxpr/psum | solution.py:119
  492.5 5.0 copy-start.3
  492.5 5.0 copy-start.2
  498.5 35.1 %copy-start.8 = (f32[128,1]{0,1:T(1,128)S(1)}, f32[128,1]{0,1:T(1,128)}, u32[]{:S(2)}) copy-start(f32[128,1]{0,1:T(1,128)} %get-tuple-element.1194) | copy-start | bytes 1540 | tf_op jit(solution)/shard_map/while
  532.1 1.5 copy-start
  535.7 7.2 %collective-permute-start.1 = (bf16[128,3072]{1,0:T(8,128)(2,1)}, bf16[128,3072]{1,0:T(8,128)(2,1)}, u32[]{:S(2)}, u32[]{:S(2)}) collective-permute-start(bf16[128,3072]{1,0:T(8,128)(2,1)} %fusion.63), channel_id=1, source_target_pairs={{2,0},{4,2},{6,4},{3,1},{5,3},{7,5},{10,8},{12,10},{14,12},{11,9},... | collective-permute-start | bytes 2359304 | tf_op jit(solution)/shard_map/while/body/eval_jaxpr/ppermute | solution.py:14
  543.1 7.0 %copy-start.4 = (bf16[128,768]{0,1:T(8,128)(2,1)S(1)}, bf16[128,768]{0,1:T(8,128)(2,1)}, u32[]{:S(2)}) copy-start(bf16[128,768]{0,1:T(8,128)(2,1)} %get-tuple-element.790) | copy-start | bytes 589828
  545.4 35.8 %all-to-all-start = ((bf16[128,4,768]{0,2,1:T(8,128)(2,1)}), bf16[128,4,768]{0,2,1:T(8,128)(2,1)S(1)}, u32[]{:S(2)}, u32[]{:S(2)}) async-start(bf16[128,4,768]{0,2,1:T(8,128)(2,1)} %bitcast.25), calls=%async_computation | async-start | bytes 1572864 | tf_op jit(solution)/shard_map/all_to_all | solution.py:141
Sparse Core Ops, SparseCore 0:
  21.9 36.0 all-reduce.2
  67.3 50.4 all-reduce.2
  127.8 51.9 all-reduce.2
  189.5 43.2 all-reduce.2
  243.5 58.2 all-reduce.4
  313.5 66.7 all-reduce.4
  394.4 64.8 all-reduce.4
  498.6 33.4 all-reduce.4
where the time goes:
time: 600 us; the launch traced here: 591 us
  waiting for transfers between devices  414 us (69%)
  other arithmetic  56.1 us (9%)
  blocking collectives  31.2 us (5%)
  matrix products  30.4 us (5%)
  local copies, waits for them, and re-layouts  23 us (4%)
  starting transfers between devices  20.6 us (3%)
  between operations  14.1 us (2%)
    psum x4, waiting for transfers between devices, backward_turn(): lax.psum(partial_dn.astype(jnp.bfloat16), 'mp').astype(jnp.float32)  224 us
    psum x4, waiting for transfers between devices, forward_turn(): proj = lax.psum(partial_proj.astype(jnp.bfloat16), 'mp').astype(jnp.float32)  190 us
    all_gather x1, blocking collectives, per_device(): lax.all_gather(attended, 'dp', axis=0, tiled=True)  31.2 us
    ppermute x8, starting transfers between devices, from_behind(): lax.ppermute(value, axis, [(source, source + steps) for source in range(l...  15.7 us
  transfers between devices with their start and end apart: 17, of which 9 were waited for; matrix products, arithmetic and copies ran while one was open for 5% of the time, Pallas kernels for 0%

commit v1 on v0

v1 whole, which is shorter than its diff:
```python
import functools
import math

import jax
import jax.numpy as jnp
from jax import lax
from jax.experimental import pallas as pl
from jax.experimental.pallas import tpu as pltpu
from jax.sharding import PartitionSpec as P

HEAD_DIM = 128
GROUPS = 2
CHUNKS = 2
MESH = pl.DeviceIdType.MESH
NT = (((1,), (1,)), ((), ()))
TN = (((0,), (0,)), ((), ()))


def dot(a, b, dims=(((1,), (0,)), ((), ()))):
    return lax.dot_general(a, b, dims, preferred_element_type=jnp.float32)


def relay_kernel(
    sizes,
    lat,
    kv,
    mask,
    wq,
    wo,
    gate,
    cot,
    out_ref,
    dx_ref,
    wg_ref,
    xbuf,
    dybuf,
    xsend,
    dxsend,
    psend,
    precv,
    bsend,
    brecv,
    own,
    prob_buf,
    qbuf,
    rbuf,
    att_all,
    dpj,
    dcol,
    s_x,
    r_x,
    s_dy,
    r_dy,
    s_p,
    r_p,
    s_b,
    r_b,
    s_att,
    r_att,
    s_dp,
    r_dp,
):
    n_dp, n_pipe, n_mp = sizes
    groups, rows, width = lat.shape
    chunks, chunk = (xbuf.shape[2], xbuf.shape[4])
    inner_width = wo.shape[0]
    heads = inner_width // HEAD_DIM
    share = dpj.shape[2]
    slabs = chunk // share
    scale = 1.0 / math.sqrt(HEAD_DIM)
    z = lax.axis_index("dp")
    p = lax.axis_index("pipe")
    y = lax.axis_index("mp")
    first = p == 0
    last = p == n_pipe - 1

    barrier = pltpu.get_barrier_semaphore()

    def greet(target):
        pl.semaphore_signal(barrier, inc=1, device_id=target, device_id_type=MESH)

    for o in range(1, n_mp):
        greet({"mp": lax.rem(y + o, n_mp)})

    @pl.loop(1, n_dp)
    def _(k):
        greet({"dp": lax.rem(z + k, n_dp)})

    @pl.when(jnp.logical_not(first))
    def _():
        for h in range(n_mp):
            greet({"pipe": p - 1, "mp": h})

    @pl.when(jnp.logical_not(last))
    def _():
        for h in range(n_mp):
            greet({"pipe": p + 1, "mp": h})

    @pl.when(first)
    def _():
        for m in range(groups):
            for h in range(n_mp):
                for c in range(chunks):
                    begin = (h * chunks + c) * chunk
                    xbuf[m, h, c] = lat[m, :, begin : begin + chunk]

    @pl.when(last)
    def _():
        for m in range(groups):
            for h in range(n_mp):
                for c in range(chunks):
                    begin = (h * chunks + c) * chunk
                    dybuf[m, h, c] = cot[m, :, begin : begin + chunk]

    edges = first.astype(jnp.int32) + last.astype(jnp.int32)
    pl.semaphore_wait(barrier, (n_mp - 1) + (n_dp - 1) + n_mp * (2 - edges))

    def group_rows(m):
        return pl.ds(pl.multiple_of(m * rows, rows), rows)

    def columns(j):
        return pl.ds(pl.multiple_of(j * chunk, 128), chunk)

    def relay_copy(src, dst, send, recv, m, c, h, target, slot):
        return pltpu.make_async_remote_copy(
            src_ref=src.at[m, c],
            dst_ref=dst.at[m, h, c],
            send_sem=send.at[m, c, slot],
            recv_sem=recv.at[m, h, c],
            device_id=target,
            device_id_type=MESH,
        )

    def forward_copy(m, c, o):
        target = {"pipe": p + 1, "mp": lax.rem(y + o, n_mp)}
        return relay_copy(xsend, xbuf, s_x, r_x, m, c, y, target, o)

    def backward_copy(m, c, o):
        target = {"pipe": p - 1, "mp": lax.rem(y + o, n_mp)}
        return relay_copy(dxsend, dybuf, s_dy, r_dy, m, c, y, target, o)

    def share_copy(src, dst, send, recv, m, c, o):
        return pltpu.make_async_remote_copy(
            src_ref=src.at[m, o - 1, c],
            dst_ref=dst.at[m, o - 1, c],
            send_sem=send.at[m, o - 1, c],
            recv_sem=recv.at[m, o - 1, c],
            device_id={"mp": lax.rem(y + o, n_mp)},
            device_id_type=MESH,
        )

    def att_copy(m, k, source):
        piece = att_all.at[source, group_rows(m)]
        return pltpu.make_async_remote_copy(
            src_ref=piece,
            dst_ref=piece,
            send_sem=s_att.at[m, k],
            recv_sem=r_att.at[m, k],
            device_id={"dp": lax.rem(z + k, n_dp)},
            device_id_type=MESH,
        )

    def dproj_copy(m, k, source, owner):
        return pltpu.make_async_remote_copy(
            src_ref=dpj.at[owner, group_rows(m)],
            dst_ref=dcol.at[source, group_rows(m)],
            send_sem=s_dp.at[m, k],
            recv_sem=r_dp.at[m, k],
            device_id={"dp": lax.rem(z + k, n_dp)},
            device_id_type=MESH,
        )

    def head(t):
        return slice(t * HEAD_DIM, (t + 1) * HEAD_DIM)

    order = [(c, o) for c in range(chunks) for o in range(n_mp)]

    def forward_send(m):
        query_raw = jnp.zeros((rows, inner_width), jnp.float32)
        squares = jnp.zeros((rows, 1), jnp.float32)
        for c, o in order:
            h = lax.rem(y + o, n_mp)

            @pl.when(jnp.logical_not(first))
            def _():
                relay_copy(xsend, xbuf, s_x, r_x, m, c, h, {"mp": y}, 0).wait_recv()

            x = xbuf[m, h, c]
            x_float = x.astype(jnp.float32)
            squares += jnp.sum(x_float * x_float, axis=-1, keepdims=True)
            query_raw += dot(x, wq[h * chunks + c])
        scale_r = lax.rsqrt(squares / width + 1e-06)
        query = (query_raw * scale_r).astype(jnp.bfloat16)
        rbuf[m] = jnp.broadcast_to(scale_r, rbuf.shape[1:])
        qbuf[m] = query
        live = mask[...] > 0
        parts = []
        for t in range(heads):
            scores = dot(query[:, head(t)], kv[0, :, head(t)], NT) * scale
            scores = jnp.where(live, scores, -1e30)
            top = jnp.max(scores, axis=-1, keepdims=True)
            powers = jnp.exp(scores - top)
            prob = powers / jnp.sum(powers, axis=-1, keepdims=True)
            prob_buf[m, t] = prob
            parts.append(dot(prob.astype(jnp.bfloat16), kv[1, :, head(t)]).astype(jnp.bfloat16))
        attended = jnp.concatenate(parts, axis=1)
        att_all[z, group_rows(m)] = attended
        for o in range(1, n_mp):
            h = lax.rem(y + o, n_mp)
            for c in range(chunks):
                piece = dot(attended, wo[:, columns(h * chunks + c)])
                psend[m, o - 1, c] = piece.astype(jnp.bfloat16)
                share_copy(psend, precv, s_p, r_p, m, c, o).start()

        @pl.loop(1, n_dp)
        def _(k):
            att_copy(m, k, z).start()

        for c in range(chunks):
            own[c] = dot(attended, wo[:, columns(y * chunks + c)])

    def forward_finish(m):
        for c in range(chunks):
            total = own[c]
            for o in range(1, n_mp):
                share_copy(psend, precv, s_p, r_p, m, c, o).wait_recv()
                total += precv[m, o - 1, c].astype(jnp.float32)
            x_float = xbuf[m, y, c].astype(jnp.float32)
            result = (x_float + gate[y * chunks + c] * total).astype(jnp.bfloat16)
            xsend[m, c] = result

            @pl.when(jnp.logical_not(last))
            def _():
                for o in reversed(range(n_mp)):
                    forward_copy(m, c, o).start()

            out_ref[m, :, c * chunk : (c + 1) * chunk] = result

    def backward_send(m):
        d_att = jnp.zeros((rows, inner_width), jnp.float32)
        for c, o in order:
            h = lax.rem(y + o, n_mp)
            j = h * chunks + c

            @pl.when(jnp.logical_not(last))
            def _():
                relay_copy(dxsend, dybuf, s_dy, r_dy, m, c, h, {"mp": y}, 0).wait_recv()

            dproj = (gate[j] * dybuf[m, h, c].astype(jnp.float32)).astype(jnp.bfloat16)
            for t in range(slabs):
                dpj[j * slabs + t, group_rows(m)] = dproj[:, t * share : (t + 1) * share]
            d_att += dot(dproj, wo[:, columns(j)], NT)

        @pl.loop(1, n_dp)
        def _(k):
            dproj_copy(m, k, z, lax.rem(z + k, n_dp)).start()

        d_att = d_att.astype(jnp.bfloat16)
        query = qbuf[m]
        inner = jnp.zeros((rows, 1), jnp.float32)
        parts = []
        for t in range(heads):
            prob = prob_buf[m, t]
            d_prob = dot(d_att[:, head(t)], kv[1, :, head(t)], NT)
            mean = jnp.sum(prob * d_prob, axis=-1, keepdims=True)
            d_score = (prob * (d_prob - mean)).astype(jnp.bfloat16)
            d_query = (dot(d_score, kv[0, :, head(t)]) * scale).astype(jnp.bfloat16)
            both = d_query.astype(jnp.float32) * query[:, head(t)].astype(jnp.float32)
            inner += jnp.sum(both, axis=-1, keepdims=True)
            parts.append(d_query)
        d_query = jnp.concatenate(parts, axis=1)
        pull = rbuf[m][:, :1] * inner / width

        def piece_of(h, c):
            x_float = xbuf[m, h, c].astype(jnp.float32)
            return dot(d_query, wq[h * chunks + c], NT) - x_float * pull

        for o in range(1, n_mp):
            h = lax.rem(y + o, n_mp)
            for c in range(chunks):
                bsend[m, o - 1, c] = piece_of(h, c).astype(jnp.bfloat16)
                share_copy(bsend, brecv, s_b, r_b, m, c, o).start()
        for c in range(chunks):
            own[c] = piece_of(y, c)

    def backward_finish(m):
        scale_r = rbuf[m][:, :1]
        for c in range(chunks):
            total = own[c]
            for o in range(1, n_mp):
                share_copy(bsend, brecv, s_b, r_b, m, c, o).wait_recv()
                total += brecv[m, o - 1, c].astype(jnp.float32)
            dy = dybuf[m, y, c].astype(jnp.float32)
            result = (dy + scale_r * total).astype(jnp.bfloat16)
            dxsend[m, c] = result

            @pl.when(jnp.logical_not(first))
            def _():
                for o in reversed(range(n_mp)):
                    backward_copy(m, c, o).start()

            dx_ref[m, :, c * chunk : (c + 1) * chunk] = result

    @pl.loop(0, groups)
    def _(m):
        forward_send(m)
        forward_finish(m)

    @pl.loop(0, groups)
    def _(m):
        backward_send(m)
        backward_finish(m)

    dcol[z] = dpj[z]

    @pl.loop(0, groups)
    def _(m):
        @pl.loop(1, n_dp)
        def _(k):
            source = lax.rem(z + n_dp - k, n_dp)
            att_copy(m, k, source).wait_recv()
            dproj_copy(m, k, source, z).wait_recv()

    depth = n_dp * groups * rows
    for t in range(heads // 2):
        cut = slice(2 * t * HEAD_DIM, 2 * (t + 1) * HEAD_DIM)
        left = att_all[:, :, cut].reshape(depth, 2 * HEAD_DIM)
        wg_ref[cut, :] = dot(left, dcol[...].reshape(depth, share), TN)

    @pl.loop(0, groups)
    def _(m):
        @pl.loop(1, n_dp)
        def _(k):
            att_copy(m, k, z).wait_send()
            dproj_copy(m, k, z, lax.rem(z + k, n_dp)).wait_send()

        for c in range(chunks):
            for o in range(1, n_mp):
                share_copy(psend, precv, s_p, r_p, m, c, o).wait_send()
                share_copy(bsend, brecv, s_b, r_b, m, c, o).wait_send()

            @pl.when(jnp.logical_not(last))
            def _():
                for o in range(n_mp):
                    forward_copy(m, c, o).wait_send()

            @pl.when(jnp.logical_not(first))
            def _():
                for o in range(n_mp):
                    backward_copy(m, c, o).wait_send()


def per_device(latents, caption_kv, caption_mask, query_weight, out_weight, gate, cotangent):
    micro, tok, width = latents.shape[1:]
    n_dp, n_pipe, n_mp = (lax.axis_size("dp"), lax.axis_size("pipe"), lax.axis_size("mp"))
    total_rows = micro * tok
    rows = total_rows // GROUPS
    half = width // n_mp
    chunk = half // CHUNKS
    inner_width = out_weight.shape[1]
    heads = inner_width // HEAD_DIM
    cap = caption_mask.shape[1]
    share = width // n_dp
    bf16, f32 = (jnp.bfloat16, jnp.float32)
    whole = (GROUPS, n_mp, CHUNKS, rows, chunk)
    mine = (GROUPS, CHUNKS, rows, chunk)
    cross = (GROUPS, n_mp - 1, CHUNKS, rows, chunk)
    sem = pltpu.SemaphoreType.DMA
    vmem = pl.BlockSpec(memory_space=pltpu.VMEM)
    section_out, input_grad, weight_grad = pl.pallas_call(
        functools.partial(relay_kernel, (n_dp, n_pipe, n_mp)),
        out_shape=(
            jax.ShapeDtypeStruct((GROUPS, rows, half), bf16),
            jax.ShapeDtypeStruct((GROUPS, rows, half), bf16),
            jax.ShapeDtypeStruct((inner_width, share), f32),
        ),
        in_specs=[vmem] * 7,
        out_specs=(vmem,) * 3,
        scratch_shapes=[
            pltpu.VMEM(whole, bf16),
            pltpu.VMEM(whole, bf16),
            pltpu.VMEM(mine, bf16),
            pltpu.VMEM(mine, bf16),
            pltpu.VMEM(cross, bf16),
            pltpu.VMEM(cross, bf16),
            pltpu.VMEM(cross, bf16),
            pltpu.VMEM(cross, bf16),
            pltpu.VMEM(mine[1:], f32),
            pltpu.VMEM((GROUPS, heads, rows, cap), f32),
            pltpu.VMEM((GROUPS, rows, inner_width), bf16),
            pltpu.VMEM((GROUPS, rows, 128), f32),
            pltpu.VMEM((n_dp, total_rows, inner_width), bf16),
            pltpu.VMEM((n_dp, total_rows, share), bf16),
            pltpu.VMEM((n_dp, total_rows, share), bf16),
            sem((GROUPS, CHUNKS, n_mp)),
            sem((GROUPS, n_mp, CHUNKS)),
            sem((GROUPS, CHUNKS, n_mp)),
            sem((GROUPS, n_mp, CHUNKS)),
            sem((GROUPS, n_mp - 1, CHUNKS)),
            sem((GROUPS, n_mp - 1, CHUNKS)),
            sem((GROUPS, n_mp - 1, CHUNKS)),
            sem((GROUPS, n_mp - 1, CHUNKS)),
            sem((GROUPS, n_dp)),
            sem((GROUPS, n_dp)),
            sem((GROUPS, n_dp)),
            sem((GROUPS, n_dp)),
        ],
        compiler_params=pltpu.CompilerParams(
            collective_id=0, has_side_effects=True, vmem_limit_bytes=56 * 2**20
        ),
        name="relay",
    )(
        latents.reshape(GROUPS, rows, width),
        caption_kv[0, 0],
        caption_mask,
        query_weight.reshape(n_mp * CHUNKS, chunk, inner_width),
        out_weight[0],
        gate.reshape(n_mp * CHUNKS, 1, chunk),
        cotangent.reshape(GROUPS, rows, width),
    )
    shape = (1, 1, micro, tok, half)
    return (section_out.reshape(shape), input_grad.reshape(shape), weight_grad[None])


def solution(mesh):
    return jax.shard_map(
        per_device,
        mesh=mesh,
        in_specs=(
            P("dp", None, None, None),
            P("dp", "pipe", None, None, "mp"),
            P("dp", None),
            P("pipe", None, "mp"),
            P("pipe", "mp", None),
            P("pipe", None),
            P("dp", None, None, None),
        ),
        out_specs=(
            P("pipe", "dp", None, None, "mp"),
            P("pipe", "dp", None, None, "mp"),
            P("pipe", "mp", "dp"),
        ),
        check_vma=False,
    )
```

time: 600 us -> 125 us (0.21); the launches traced: 591 us -> 125 us
  waiting for transfers between devices: 414 us -> 0 us
  Pallas kernels: 0 us -> 117 us
  other arithmetic: 56.1 us -> 0 us
  blocking collectives: 31.2 us -> 0 us
  matrix products: 30.4 us -> 0 us
  starting transfers between devices: 20.6 us -> 0 us
  local copies, waits for them, and re-layouts: 23 us -> 6.75 us
  between operations: 14.1 us -> 0.64 us
    psum x8 -> x0, waiting for transfers between devices: 414 us -> none  [the longest x4 224 us: backward_turn(): lax.psum(partial_dn.astype(jnp.bfloat16), 'mp').astype(jnp.float32)]
    pallas_call x0 -> x1, Pallas kernels: none -> 117 us  [per_device(): pl.pallas_call(functools.partial(relay_kernel, (n_dp, n_pipe, n_mp)), out...]
    all_gather x1 -> x0, blocking collectives: 31.2 us -> none  [per_device(): lax.all_gather(attended, 'dp', axis=0, tiled=True)]
    select_n x24 -> x0, other arithmetic: 30.8 us -> none  [the longest x4 7.69 us: backward_turn(): grad_in = jnp.where(mine, dx_share, grad_in)]
    dot_general x9 -> x0, matrix products: 24.6 us -> none  [the longest x2 7.02 us: forward_parts(): jnp.dot(normed, w_query, preferred_element_type=jnp.float32)]
    ppermute x8 -> x0, starting transfers between devices: 15.7 us -> none  [from_behind(): lax.ppermute(value, axis, [(source, source + steps) for source in range(l...]
    convert_element_type x11 -> x0, other arithmetic: 14.2 us -> none  [the longest x4 8.5 us: backward_turn(): dx = (incoming.astype(jnp.float32) + scale_r * (dnormed - x_float * (scal...]
    another operation x12 -> x0, local copies, waits for them, and re-layouts: 8.24 us -> none
  transfers between devices with their start and end apart: 17 -> 0, of which waited for: 9 -> 0; matrix products, arithmetic and copies ran while one was open for 5% -> 0% of each run, Pallas kernels for 0% -> 0%
where the time goes in v1:
time: 125 us
  Pallas kernels  117 us (94%)
  local copies, waits for them, and re-layouts  6.75 us (5%)
    pallas_call x1, Pallas kernels, per_device(): pl.pallas_call(functools.partial(relay_kernel, (n_dp, n_pipe, n_mp)), out...  117 us
    unnamed x3, local copies, waits for them, and re-layouts  6.75 us

profile of v1, /device:TPU:0, one launch (start us, length us, event | category | flops | bytes accessed | tf_op | source)
XLA Modules:
  0.0 124.9 jit_solution(1604361398455387820)
XLA Ops:
  0.6 117.5 %relay.1 = (bf16[2,64,1536]{2,1,0:T(8,128)(2,1)}, bf16[2,64,1536]{2,1,0:T(8,128)(2,1)}, f32[768,768]{1,0:T(8,128)}) custom-call(bf16[2,64,3072]{2,1,0:T(8,128)(2,1)} %bitcast.12, bf16[2,128,768]{2,1,0:T(8,128)(2,1)} %bitcast.14, s32[1,128]{1,0:T(1,128)} %mask.1, bf16[4,768,768]{2,1,0:T(8,128)(2,1)} %bitcast.9, bf16[768,3072]{1,0:T(8,128)(2,1)} %bitcast.10, ...), custom_call_target="tpu_custom_call" | custom-call | tf_op jit(solution)/shard_map/relay/pallas_call | solution.py:370
  118.1 1.8 %copy.13 = bf16[1,1,2,64,1536]{4,3,2,1,0:T(8,128)(2,1)} copy(bf16[1,1,2,64,1536]{4,3,2,1,0:T(8,128)(2,1)} %bitcast.16) | data formatting | bytes 786432
  119.9 1.8 %copy.14 = bf16[1,1,2,64,1536]{4,3,2,1,0:T(8,128)(2,1)} copy(bf16[1,1,2,64,1536]{4,3,2,1,0:T(8,128)(2,1)} %bitcast.15) | data formatting | bytes 786432
  121.6 3.2 %copy.15 = f32[1,768,768]{2,1,0:T(8,128)} copy(f32[1,768,768]{2,1,0:T(8,128)} %bitcast.11) | data formatting | bytes 4718592

commit v2 on v1

--- a/solution.py
+++ b/solution.py
@@ -23,15 +23,19 @@
 def relay_kernel(
     sizes,
     lat,
-    kv,
+    kv_any,
     mask,
-    wq,
-    wo,
+    wq_any,
+    wo_any,
     gate,
     cot,
     out_ref,
     dx_ref,
-    wg_ref,
+    att_all,
+    dcol,
+    kv,
+    wq,
+    wo,
     xbuf,
     dybuf,
     xsend,
@@ -44,9 +48,10 @@
     prob_buf,
     qbuf,
     rbuf,
-    att_all,
+    dqbuf,
+    pbuf,
     dpj,
-    dcol,
+    s_w,
     s_x,
     r_x,
     s_dy,
@@ -74,6 +79,34 @@
     first = p == 0
     last = p == n_pipe - 1
 
+    def load(i, src, dst):
+        return pltpu.make_async_copy(src, dst, s_w.at[i])
+
+    load_wq = load(0, wq_any, wq)
+    load_kv = load(1, kv_any, kv)
+    load_wo = load(2, wo_any, wo)
+
+    def load_rows(src, dst, sems):
+        for m in range(groups):
+            for c in range(chunks):
+                for h in range(n_mp):
+                    begin = (h * chunks + c) * chunk
+                    pltpu.make_async_copy(
+                        src.at[m, :, pl.ds(begin, chunk)], dst.at[m, h, c], sems.at[m, h, c]
+                    ).start()
+
+    @pl.when(first)
+    def _():
+        load_rows(lat, xbuf, r_x)
+
+    load_wq.start()
+    load_kv.start()
+    load_wo.start()
+
+    @pl.when(last)
+    def _():
+        load_rows(cot, dybuf, r_dy)
+
     barrier = pltpu.get_barrier_semaphore()
 
     def greet(target):
@@ -95,22 +128,6 @@
     def _():
         for h in range(n_mp):
             greet({"pipe": p + 1, "mp": h})
-
-    @pl.when(first)
-    def _():
-        for m in range(groups):
-            for h in range(n_mp):
-                for c in range(chunks):
-                    begin = (h * chunks + c) * chunk
-                    xbuf[m, h, c] = lat[m, :, begin : begin + chunk]
-
-    @pl.when(last)
-    def _():
-        for m in range(groups):
-            for h in range(n_mp):
-                for c in range(chunks):
-                    begin = (h * chunks + c) * chunk
-                    dybuf[m, h, c] = cot[m, :, begin : begin + chunk]
 
     edges = first.astype(jnp.int32) + last.astype(jnp.int32)
     pl.semaphore_wait(barrier, (n_mp - 1) + (n_dp - 1) + n_mp * (2 - edges))
@@ -175,16 +192,13 @@
 
     order = [(c, o) for c in range(chunks) for o in range(n_mp)]
 
-    def forward_send(m):
+    def forward_query(m):
         query_raw = jnp.zeros((rows, inner_width), jnp.float32)
         squares = jnp.zeros((rows, 1), jnp.float32)
         for c, o in order:
             h = lax.rem(y + o, n_mp)
 
-            @pl.when(jnp.logical_not(first))
-            def _():
-                relay_copy(xsend, xbuf, s_x, r_x, m, c, h, {"mp": y}, 0).wait_recv()
-
+            relay_copy(xsend, xbuf, s_x, r_x, m, c, h, {"mp": y}, 0).wait_recv()
             x = xbuf[m, h, c]
             x_float = x.astype(jnp.float32)
             squares += jnp.sum(x_float * x_float, axis=-1, keepdims=True)
@@ -205,23 +219,25 @@
             parts.append(dot(prob.astype(jnp.bfloat16), kv[1, :, head(t)]).astype(jnp.bfloat16))
         attended = jnp.concatenate(parts, axis=1)
         att_all[z, group_rows(m)] = attended
+
+        @pl.loop(1, n_dp)
+        def _(k):
+            att_copy(m, k, z).start()
+
+    def forward_share(m):
+        attended = att_all[z, group_rows(m)]
         for o in range(1, n_mp):
             h = lax.rem(y + o, n_mp)
             for c in range(chunks):
                 piece = dot(attended, wo[:, columns(h * chunks + c)])
                 psend[m, o - 1, c] = piece.astype(jnp.bfloat16)
                 share_copy(psend, precv, s_p, r_p, m, c, o).start()
-
-        @pl.loop(1, n_dp)
-        def _(k):
-            att_copy(m, k, z).start()
-
         for c in range(chunks):
-            own[c] = dot(attended, wo[:, columns(y * chunks + c)])
+            own[0, m, c] = dot(attended, wo[:, columns(y * chunks + c)])
 
     def forward_finish(m):
         for c in range(chunks):
-            total = own[c]
+            total = own[0, m, c]
             for o in range(1, n_mp):
                 share_copy(psend, precv, s_p, r_p, m, c, o).wait_recv()
                 total += precv[m, o - 1, c].astype(jnp.float32)
@@ -236,16 +252,13 @@
 
             out_ref[m, :, c * chunk : (c + 1) * chunk] = result
 
-    def backward_send(m):
+    def backward_query(m):
         d_att = jnp.zeros((rows, inner_width), jnp.float32)
         for c, o in order:
             h = lax.rem(y + o, n_mp)
             j = h * chunks + c
 
-            @pl.when(jnp.logical_not(last))
-            def _():
-                relay_copy(dxsend, dybuf, s_dy, r_dy, m, c, h, {"mp": y}, 0).wait_recv()
-
+            relay_copy(dxsend, dybuf, s_dy, r_dy, m, c, h, {"mp": y}, 0).wait_recv()
             dproj = (gate[j] * dybuf[m, h, c].astype(jnp.float32)).astype(jnp.bfloat16)
             for t in range(slabs):
                 dpj[j * slabs + t, group_rows(m)] = dproj[:, t * share : (t + 1) * share]
@@ -268,8 +281,12 @@
             both = d_query.astype(jnp.float32) * query[:, head(t)].astype(jnp.float32)
             inner += jnp.sum(both, axis=-1, keepdims=True)
             parts.append(d_query)
-        d_query = jnp.concatenate(parts, axis=1)
-        pull = rbuf[m][:, :1] * inner / width
+        dqbuf[m] = jnp.concatenate(parts, axis=1)
+        pbuf[m] = jnp.broadcast_to(rbuf[m][:, :1] * inner / width, pbuf.shape[1:])
+
+    def backward_share(m):
+        d_query = dqbuf[m]
+        pull = pbuf[m][:, :1]
 
         def piece_of(h, c):
             x_float = xbuf[m, h, c].astype(jnp.float32)
@@ -281,12 +298,12 @@
                 bsend[m, o - 1, c] = piece_of(h, c).astype(jnp.bfloat16)
                 share_copy(bsend, brecv, s_b, r_b, m, c, o).start()
         for c in range(chunks):
-            own[c] = piece_of(y, c)
+            own[1, m, c] = piece_of(y, c)
 
     def backward_finish(m):
         scale_r = rbuf[m][:, :1]
         for c in range(chunks):
-            total = own[c]
+            total = own[1, m, c]
             for o in range(1, n_mp):
                 share_copy(bsend, brecv, s_b, r_b, m, c, o).wait_recv()
                 total += brecv[m, o - 1, c].astype(jnp.float32)
@@ -301,15 +318,31 @@
 
             dx_ref[m, :, c * chunk : (c + 1) * chunk] = result
 
-    @pl.loop(0, groups)
-    def _(m):
-        forward_send(m)
-        forward_finish(m)
-
-    @pl.loop(0, groups)
-    def _(m):
-        backward_send(m)
-        backward_finish(m)
+    late = last.astype(jnp.int32)
+    turn = groups * (1 - late)
+    held_back = (groups + 1) * late
+
+    load_wq.wait()
+    load_kv.wait()
+
+    @pl.loop(0, 2 * groups + 2)
+    def _(step):
+        def phase(run, m):
+            @pl.when(jnp.logical_and(m >= 0, m < groups))
+            def _():
+                run(m)
+
+        phase(forward_query, step)
+
+        @pl.when(step == 0)
+        def _():
+            load_wo.wait()
+
+        phase(forward_finish, step - held_back - 1)
+        phase(forward_share, step - held_back)
+        phase(backward_query, step - turn)
+        phase(backward_finish, step - turn - 1)
+        phase(backward_share, step - turn)
 
     dcol[z] = dpj[z]
 
@@ -321,12 +354,6 @@
             att_copy(m, k, source).wait_recv()
             dproj_copy(m, k, source, z).wait_recv()
 
-    depth = n_dp * groups * rows
-    for t in range(heads // 2):
-        cut = slice(2 * t * HEAD_DIM, 2 * (t + 1) * HEAD_DIM)
-        left = att_all[:, :, cut].reshape(depth, 2 * HEAD_DIM)
-        wg_ref[cut, :] = dot(left, dcol[...].reshape(depth, share), TN)
-
     @pl.loop(0, groups)
     def _(m):
         @pl.loop(1, n_dp)
@@ -348,6 +375,14 @@
             def _():
                 for o in range(n_mp):
                     backward_copy(m, c, o).wait_send()
+
+
+def result_kernel(att, dproj, out, dx, out_ref, dx_ref, wg_ref):
+    depth = att.shape[0] * att.shape[1]
+    left = att[...].reshape(depth, att.shape[2])
+    wg_ref[...] = dot(left, dproj[...].reshape(depth, dproj.shape[2]), TN)
+    out_ref[...] = out[...]
+    dx_ref[...] = dx[...]
 
 
 def per_device(latents, caption_kv, caption_mask, query_weight, out_weight, gate, cotangent):
@@ -367,16 +402,21 @@
     cross = (GROUPS, n_mp - 1, CHUNKS, rows, chunk)
     sem = pltpu.SemaphoreType.DMA
     vmem = pl.BlockSpec(memory_space=pltpu.VMEM)
-    section_out, input_grad, weight_grad = pl.pallas_call(
+    anywhere = pl.BlockSpec(memory_space=pl.ANY)
+    section_out, input_grad, attended, dproj = pl.pallas_call(
         functools.partial(relay_kernel, (n_dp, n_pipe, n_mp)),
         out_shape=(
             jax.ShapeDtypeStruct((GROUPS, rows, half), bf16),
             jax.ShapeDtypeStruct((GROUPS, rows, half), bf16),
-            jax.ShapeDtypeStruct((inner_width, share), f32),
+            jax.ShapeDtypeStruct((n_dp, total_rows, inner_width), bf16),
+            jax.ShapeDtypeStruct((n_dp, total_rows, share), bf16),
         ),
-        in_specs=[vmem] * 7,
-        out_specs=(vmem,) * 3,
+        in_specs=[anywhere, anywhere, vmem, anywhere, anywhere, vmem, anywhere],
+        out_specs=(vmem,) * 4,
         scratch_shapes=[
+            pltpu.VMEM(caption_kv.shape[2:], bf16),
+            pltpu.VMEM((n_mp * CHUNKS, chunk, inner_width), bf16),
+            pltpu.VMEM(out_weight.shape[1:], bf16),
             pltpu.VMEM(whole, bf16),
             pltpu.VMEM(whole, bf16),
             pltpu.VMEM(mine, bf16),
@@ -385,13 +425,14 @@
             pltpu.VMEM(cross, bf16),
             pltpu.VMEM(cross, bf16),
             pltpu.VMEM(cross, bf16),
-            pltpu.VMEM(mine[1:], f32),
+            pltpu.VMEM((2,) + mine, f32),
             pltpu.VMEM((GROUPS, heads, rows, cap), f32),
             pltpu.VMEM((GROUPS, rows, inner_width), bf16),
             pltpu.VMEM((GROUPS, rows, 128), f32),
-            pltpu.VMEM((n_dp, total_rows, inner_width), bf16),
+            pltpu.VMEM((GROUPS, rows, inner_width), bf16),
+            pltpu.VMEM((GROUPS, rows, 128), f32),
             pltpu.VMEM((n_dp, total_rows, share), bf16),
-            pltpu.VMEM((n_dp, total_rows, share), bf16),
+            sem((3,)),
             sem((GROUPS, CHUNKS, n_mp)),
             sem((GROUPS, n_mp, CHUNKS)),
             sem((GROUPS, CHUNKS, n_mp)),
@@ -418,6 +459,27 @@
         gate.reshape(n_mp * CHUNKS, 1, chunk),
         cotangent.reshape(GROUPS, rows, width),
     )
+    tiles = heads // 2 if heads % 2 == 0 and half % (heads // 2 * 128) == 0 else 1
+    part = inner_width // tiles
+    band = pl.BlockSpec((GROUPS, rows, half // tiles), lambda i: (0, 0, i))
+    section_out, input_grad, weight_grad = pl.pallas_call(
+        result_kernel,
+        grid=(tiles,),
+        out_shape=(
+            jax.ShapeDtypeStruct((GROUPS, rows, half), bf16),
+            jax.ShapeDtypeStruct((GROUPS, rows, half), bf16),
+            jax.ShapeDtypeStruct((inner_width, share), f32),
+        ),
+        in_specs=[
+            pl.BlockSpec((n_dp, total_rows, part), lambda i: (0, 0, i)),
+            pl.BlockSpec((n_dp, total_rows, share), lambda i: (0, 0, 0)),
+            band,
+            band,
+        ],
+        out_specs=(band, band, pl.BlockSpec((part, share), lambda i: (i, 0))),
+        compiler_params=pltpu.CompilerParams(vmem_limit_bytes=56 * 2**20),
+        name="results",
+    )(attended, dproj, section_out, input_grad)
     shape = (1, 1, micro, tok, half)
     return (section_out.reshape(shape), input_grad.reshape(shape), weight_grad[None])
 

time: 125 us -> 111 us (0.89)
  Pallas kernels: 117 us -> 110 us
  local copies, waits for them, and re-layouts: 6.75 us -> 0 us
    pallas_call x1, Pallas kernels: 117 us -> 105 us  [per_device(): pl.pallas_call(functools.partial(relay_kernel, (n_dp, n_pipe, n_mp)), out...]
    unnamed x3 -> x0, local copies, waits for them, and re-layouts: 6.75 us -> none
    pallas_call x0 -> x1, Pallas kernels: none -> 4.71 us  [per_device(): pl.pallas_call(result_kernel, grid=(tiles,), out_shape=(jax.ShapeDtypeStr...]
where the time goes in v2:
time: 111 us; the launch traced here: 110 us
  Pallas kernels  110 us (99%)
    pallas_call x1, Pallas kernels, per_device(): pl.pallas_call(functools.partial(relay_kernel, (n_dp, n_pipe, n_mp)), out...  105 us
    pallas_call x1, Pallas kernels, per_device(): pl.pallas_call(result_kernel, grid=(tiles,), out_shape=(jax.ShapeDtypeStr...  4.71 us

profile of v2, /device:TPU:0, one launch (start us, length us, event | category | flops | bytes accessed | tf_op | source)
XLA Modules:
  0.0 110.4 jit_solution(14806443108086987384)
XLA Ops:
  0.6 105.0 %relay.1 = (bf16[2,64,1536]{2,1,0:T(8,128)(2,1)}, bf16[2,64,1536]{2,1,0:T(8,128)(2,1)}, bf16[4,128,768]{2,1,0:T(8,128)(2,1)}, bf16[4,128,768]{2,1,0:T(8,128)(2,1)}) custom-call(bf16[2,64,3072]{2,1,0:T(8,128)(2,1)} %bitcast.11, bf16[2,128,768]{2,1,0:T(8,128)(2,1)} %bitcast.13, s32[1,128]{1,0:T(1,128)} %mask.1, bf16[4,768,768]{2,1,0:T(8,128)(2,1)} %bitcast.9, ...), custom_call_target="tpu_custom_call" | custom-call | tf_op jit(solution)/shard_map/relay/pallas_call | solution.py:406
  105.7 4.7 %results.1 = (bf16[2,64,1536]{2,1,0:T(8,128)(2,1)}, bf16[2,64,1536]{2,1,0:T(8,128)(2,1)}, f32[768,768]{1,0:T(8,128)}) custom-call(bf16[4,128,768]{2,1,0:T(8,128)(2,1)} %get-tuple-element.10.att, bf16[4,128,768]{2,1,0:T(8,128)(2,1)} %get-tuple-element.11.dproj, bf16[2,64,1536]{2,1,0:T(8,128)(2,1)} %get-tuple-element.12.out, ...), custom_call_target="tpu_custom_call" | custom-call | tf_op jit(solution)/shard_map/results/pallas_call | solution.py:465

commit v3 on v2

--- a/solution.py
+++ b/solution.py
@@ -9,7 +9,7 @@
 from jax.sharding import PartitionSpec as P
 
 HEAD_DIM = 128
-GROUPS = 2
+GROUPS = 4
 CHUNKS = 2
 MESH = pl.DeviceIdType.MESH
 NT = (((1,), (1,)), ((), ()))

time: 111 us -> 116 us (1.045)
  Pallas kernels: 110 us -> 115 us
    pallas_call x1, Pallas kernels: 105 us -> 110 us  [per_device(): pl.pallas_call(functools.partial(relay_kernel, (n_dp, n_pipe, n_mp)), out...]
where the time goes in v3:
time: 116 us
  Pallas kernels  115 us (99%)
    pallas_call x1, Pallas kernels, per_device(): pl.pallas_call(functools.partial(relay_kernel, (n_dp, n_pipe, n_mp)), out...  110 us
    pallas_call x1, Pallas kernels, per_device(): pl.pallas_call(result_kernel, grid=(tiles,), out_shape=(jax.ShapeDtypeStr...  4.71 us

profile of v3, /device:TPU:0, one launch (start us, length us, event | category | flops | bytes accessed | tf_op | source)
XLA Modules:
  0.0 115.6 jit_solution(6155982090591894834)
XLA Ops:
  0.6 110.3 %relay.1 = (bf16[4,32,1536]{2,1,0:T(8,128)(2,1)}, bf16[4,32,1536]{2,1,0:T(8,128)(2,1)}, bf16[4,128,768]{2,1,0:T(8,128)(2,1)}, bf16[4,128,768]{2,1,0:T(8,128)(2,1)}) custom-call(bf16[4,32,3072]{2,1,0:T(8,128)(2,1)} %bitcast.11, bf16[2,128,768]{2,1,0:T(8,128)(2,1)} %bitcast.13, s32[1,128]{1,0:T(1,128)} %mask.1, bf16[4,768,768]{2,1,0:T(8,128)(2,1)} %bitcast.9, ...), custom_call_target="tpu_custom_call" | custom-call | tf_op jit(solution)/shard_map/relay/pallas_call | solution.py:406
  110.9 4.7 %results.1 = (bf16[4,32,1536]{2,1,0:T(8,128)(2,1)}, bf16[4,32,1536]{2,1,0:T(8,128)(2,1)}, f32[768,768]{1,0:T(8,128)}) custom-call(bf16[4,128,768]{2,1,0:T(8,128)(2,1)} %get-tuple-element.10.att, bf16[4,128,768]{2,1,0:T(8,128)(2,1)} %get-tuple-element.11.dproj, bf16[4,32,1536]{2,1,0:T(8,128)(2,1)} %get-tuple-element.12.out, ...), custom_call_target="tpu_custom_call" | custom-call | tf_op jit(solution)/shard_map/results/pallas_call | solution.py:465

commit v4 on v2

--- a/solution.py
+++ b/solution.py
@@ -22,6 +22,7 @@
 
 def relay_kernel(
     sizes,
+    tiles,
     lat,
     kv_any,
     mask,
@@ -31,8 +32,12 @@
     cot,
     out_ref,
     dx_ref,
+    wg_ref,
     att_all,
     dcol,
+    wg_vmem,
+    wqt,
+    wot,
     kv,
     wq,
     wo,
@@ -52,6 +57,7 @@
     pbuf,
     dpj,
     s_w,
+    s_g,
     s_x,
     r_x,
     s_dy,
@@ -190,39 +196,35 @@
     def head(t):
         return slice(t * HEAD_DIM, (t + 1) * HEAD_DIM)
 
+    def fold(values):
+        pieces = [values[:, i : i + 128] for i in range(0, values.shape[1], 128)]
+        return functools.reduce(jnp.add, pieces)
+
     order = [(c, o) for c in range(chunks) for o in range(n_mp)]
 
     def forward_query(m):
         query_raw = jnp.zeros((rows, inner_width), jnp.float32)
-        squares = jnp.zeros((rows, 1), jnp.float32)
+        squares = jnp.zeros((rows, 128), jnp.float32)
         for c, o in order:
             h = lax.rem(y + o, n_mp)
-
             relay_copy(xsend, xbuf, s_x, r_x, m, c, h, {"mp": y}, 0).wait_recv()
             x = xbuf[m, h, c]
-            x_float = x.astype(jnp.float32)
-            squares += jnp.sum(x_float * x_float, axis=-1, keepdims=True)
             query_raw += dot(x, wq[h * chunks + c])
+            squares += fold(jnp.square(x.astype(jnp.float32)))
+        squares = jnp.sum(squares, axis=-1, keepdims=True)
         scale_r = lax.rsqrt(squares / width + 1e-06)
         query = (query_raw * scale_r).astype(jnp.bfloat16)
         rbuf[m] = jnp.broadcast_to(scale_r, rbuf.shape[1:])
         qbuf[m] = query
         live = mask[...] > 0
-        parts = []
-        for t in range(heads):
-            scores = dot(query[:, head(t)], kv[0, :, head(t)], NT) * scale
-            scores = jnp.where(live, scores, -1e30)
-            top = jnp.max(scores, axis=-1, keepdims=True)
-            powers = jnp.exp(scores - top)
-            prob = powers / jnp.sum(powers, axis=-1, keepdims=True)
-            prob_buf[m, t] = prob
-            parts.append(dot(prob.astype(jnp.bfloat16), kv[1, :, head(t)]).astype(jnp.bfloat16))
-        attended = jnp.concatenate(parts, axis=1)
-        att_all[z, group_rows(m)] = attended
-
-        @pl.loop(1, n_dp)
-        def _(k):
-            att_copy(m, k, z).start()
+        scores = jnp.stack([dot(query[:, head(t)], kv[0, :, head(t)], NT) for t in range(heads)])
+        scores = jnp.where(live[None], scores * scale, -1e30)
+        powers = jnp.exp(scores - jnp.max(scores, axis=-1, keepdims=True))
+        prob = powers * (1.0 / jnp.sum(powers, axis=-1, keepdims=True))
+        prob_buf[m] = prob
+        probs = prob.astype(jnp.bfloat16)
+        parts = [dot(probs[t], kv[1, :, head(t)]).astype(jnp.bfloat16) for t in range(heads)]
+        att_all[z, group_rows(m)] = jnp.concatenate(parts, axis=1)
 
     def forward_share(m):
         attended = att_all[z, group_rows(m)]
@@ -235,6 +237,10 @@
         for c in range(chunks):
             own[0, m, c] = dot(attended, wo[:, columns(y * chunks + c)])
 
+        @pl.loop(1, n_dp)
+        def _(k):
+            att_copy(m, k, z).start()
+
     def forward_finish(m):
         for c in range(chunks):
             total = own[0, m, c]
@@ -262,26 +268,18 @@
             dproj = (gate[j] * dybuf[m, h, c].astype(jnp.float32)).astype(jnp.bfloat16)
             for t in range(slabs):
                 dpj[j * slabs + t, group_rows(m)] = dproj[:, t * share : (t + 1) * share]
-            d_att += dot(dproj, wo[:, columns(j)], NT)
-
-        @pl.loop(1, n_dp)
-        def _(k):
-            dproj_copy(m, k, z, lax.rem(z + k, n_dp)).start()
+            d_att += dot(dproj, wot[j])
 
         d_att = d_att.astype(jnp.bfloat16)
-        query = qbuf[m]
-        inner = jnp.zeros((rows, 1), jnp.float32)
-        parts = []
-        for t in range(heads):
-            prob = prob_buf[m, t]
-            d_prob = dot(d_att[:, head(t)], kv[1, :, head(t)], NT)
-            mean = jnp.sum(prob * d_prob, axis=-1, keepdims=True)
-            d_score = (prob * (d_prob - mean)).astype(jnp.bfloat16)
-            d_query = (dot(d_score, kv[0, :, head(t)]) * scale).astype(jnp.bfloat16)
-            both = d_query.astype(jnp.float32) * query[:, head(t)].astype(jnp.float32)
-            inner += jnp.sum(both, axis=-1, keepdims=True)
-            parts.append(d_query)
-        dqbuf[m] = jnp.concatenate(parts, axis=1)
+        prob = prob_buf[m]
+        d_prob = jnp.stack([dot(d_att[:, head(t)], kv[1, :, head(t)], NT) for t in range(heads)])
+        mean = jnp.sum(prob * d_prob, axis=-1, keepdims=True)
+        d_score = (prob * (d_prob - mean)).astype(jnp.bfloat16)
+        parts = [dot(d_score[t], kv[0, :, head(t)]) for t in range(heads)]
+        d_query = (jnp.concatenate(parts, axis=1) * scale).astype(jnp.bfloat16)
+        dqbuf[m] = d_query
+        both = d_query.astype(jnp.float32) * qbuf[m].astype(jnp.float32)
+        inner = jnp.sum(fold(both), axis=-1, keepdims=True)
         pbuf[m] = jnp.broadcast_to(rbuf[m][:, :1] * inner / width, pbuf.shape[1:])
 
     def backward_share(m):
@@ -290,7 +288,7 @@
 
         def piece_of(h, c):
             x_float = xbuf[m, h, c].astype(jnp.float32)
-            return dot(d_query, wq[h * chunks + c], NT) - x_float * pull
+            return dot(d_query, wqt[h * chunks + c]) - x_float * pull
 
         for o in range(1, n_mp):
             h = lax.rem(y + o, n_mp)
@@ -299,6 +297,10 @@
                 share_copy(bsend, brecv, s_b, r_b, m, c, o).start()
         for c in range(chunks):
             own[1, m, c] = piece_of(y, c)
+
+        @pl.loop(1, n_dp)
+        def _(k):
+            dproj_copy(m, k, z, lax.rem(z + k, n_dp)).start()
 
     def backward_finish(m):
         scale_r = rbuf[m][:, :1]
@@ -322,10 +324,39 @@
     turn = groups * (1 - late)
     held_back = (groups + 1) * late
 
+    def turn_weights():
+        @pl.loop(0, n_mp * chunks)
+        def _(j):
+            wqt[j] = wq[j].T
+            wot[j] = wo[:, columns(j)].T
+
+    def weight_grad():
+        dcol[z] = dpj[z]
+
+        @pl.loop(0, groups)
+        def _(m):
+            @pl.loop(1, n_dp)
+            def _(k):
+                source = lax.rem(z + n_dp - k, n_dp)
+                att_copy(m, k, source).wait_recv()
+                dproj_copy(m, k, source, z).wait_recv()
+
+        depth = n_dp * groups * rows
+        right = dcol[...].reshape(depth, share)
+        for i in range(tiles):
+            cut = slice(i * (inner_width // tiles), (i + 1) * (inner_width // tiles))
+            left = att_all[:, :, cut].reshape(depth, inner_width // tiles)
+            wg_vmem[cut, :] = dot(left, right, TN)
+            keep_grad(i).start()
+
+    def keep_grad(i):
+        cut = pl.ds(i * (inner_width // tiles), inner_width // tiles)
+        return pltpu.make_async_copy(wg_vmem.at[cut], wg_ref.at[cut], s_g.at[i])
+
     load_wq.wait()
     load_kv.wait()
 
-    @pl.loop(0, 2 * groups + 2)
+    @pl.loop(-1, 2 * groups + 3)
     def _(step):
         def phase(run, m):
             @pl.when(jnp.logical_and(m >= 0, m < groups))
@@ -334,25 +365,28 @@
 
         phase(forward_query, step)
 
-        @pl.when(step == 0)
+        @pl.when(step == jnp.where(first, 0, -1))
         def _():
             load_wo.wait()
 
         phase(forward_finish, step - held_back - 1)
         phase(forward_share, step - held_back)
+
+        @pl.when(step == jnp.where(first, groups, -1))
+        def _():
+            turn_weights()
+
         phase(backward_query, step - turn)
+
+        @pl.when(step == jnp.where(first, 2 * groups, 2 * groups + 2))
+        def _():
+            weight_grad()
+
         phase(backward_finish, step - turn - 1)
         phase(backward_share, step - turn)
 
-    dcol[z] = dpj[z]
-
-    @pl.loop(0, groups)
-    def _(m):
-        @pl.loop(1, n_dp)
-        def _(k):
-            source = lax.rem(z + n_dp - k, n_dp)
-            att_copy(m, k, source).wait_recv()
-            dproj_copy(m, k, source, z).wait_recv()
+    for i in range(tiles):
+        keep_grad(i).wait()
 
     @pl.loop(0, groups)
     def _(m):
@@ -377,12 +411,10 @@
                     backward_copy(m, c, o).wait_send()
 
 
-def result_kernel(att, dproj, out, dx, out_ref, dx_ref, wg_ref):
-    depth = att.shape[0] * att.shape[1]
-    left = att[...].reshape(depth, att.shape[2])
-    wg_ref[...] = dot(left, dproj[...].reshape(depth, dproj.shape[2]), TN)
+def result_kernel(out, dx, wg, out_ref, dx_ref, wg_ref):
     out_ref[...] = out[...]
     dx_ref[...] = dx[...]
+    wg_ref[...] = wg[...]
 
 
 def per_device(latents, caption_kv, caption_mask, query_weight, out_weight, gate, cotangent):
@@ -402,18 +434,24 @@
     cross = (GROUPS, n_mp - 1, CHUNKS, rows, chunk)
     sem = pltpu.SemaphoreType.DMA
     vmem = pl.BlockSpec(memory_space=pltpu.VMEM)
+    tiles = heads // 2 if heads % 2 == 0 and half % (heads // 2 * 128) == 0 else 1
+    part = inner_width // tiles
     anywhere = pl.BlockSpec(memory_space=pl.ANY)
-    section_out, input_grad, attended, dproj = pl.pallas_call(
-        functools.partial(relay_kernel, (n_dp, n_pipe, n_mp)),
+    section_out, input_grad, weight_grad = pl.pallas_call(
+        functools.partial(relay_kernel, (n_dp, n_pipe, n_mp), tiles),
         out_shape=(
             jax.ShapeDtypeStruct((GROUPS, rows, half), bf16),
             jax.ShapeDtypeStruct((GROUPS, rows, half), bf16),
-            jax.ShapeDtypeStruct((n_dp, total_rows, inner_width), bf16),
-            jax.ShapeDtypeStruct((n_dp, total_rows, share), bf16),
+            jax.ShapeDtypeStruct((inner_width, share), f32),
         ),
         in_specs=[anywhere, anywhere, vmem, anywhere, anywhere, vmem, anywhere],
-        out_specs=(vmem,) * 4,
+        out_specs=(vmem, vmem, anywhere),
         scratch_shapes=[
+            pltpu.VMEM((n_dp, total_rows, inner_width), bf16),
+            pltpu.VMEM((n_dp, total_rows, share), bf16),
+            pltpu.VMEM((inner_width, share), f32),
+            pltpu.VMEM((n_mp * CHUNKS, inner_width, chunk), bf16),
+            pltpu.VMEM((n_mp * CHUNKS, chunk, inner_width), bf16),
             pltpu.VMEM(caption_kv.shape[2:], bf16),
             pltpu.VMEM((n_mp * CHUNKS, chunk, inner_width), bf16),
             pltpu.VMEM(out_weight.shape[1:], bf16),
@@ -433,6 +471,7 @@
             pltpu.VMEM((GROUPS, rows, 128), f32),
             pltpu.VMEM((n_dp, total_rows, share), bf16),
             sem((3,)),
+            sem((tiles,)),
             sem((GROUPS, CHUNKS, n_mp)),
             sem((GROUPS, n_mp, CHUNKS)),
             sem((GROUPS, CHUNKS, n_mp)),
@@ -459,9 +498,8 @@
         gate.reshape(n_mp * CHUNKS, 1, chunk),
         cotangent.reshape(GROUPS, rows, width),
     )
-    tiles = heads // 2 if heads % 2 == 0 and half % (heads // 2 * 128) == 0 else 1
-    part = inner_width // tiles
     band = pl.BlockSpec((GROUPS, rows, half // tiles), lambda i: (0, 0, i))
+    grad_band = pl.BlockSpec((part, share), lambda i: (i, 0))
     section_out, input_grad, weight_grad = pl.pallas_call(
         result_kernel,
         grid=(tiles,),
@@ -470,16 +508,11 @@
             jax.ShapeDtypeStruct((GROUPS, rows, half), bf16),
             jax.ShapeDtypeStruct((inner_width, share), f32),
         ),
-        in_specs=[
-            pl.BlockSpec((n_dp, total_rows, part), lambda i: (0, 0, i)),
-            pl.BlockSpec((n_dp, total_rows, share), lambda i: (0, 0, 0)),
-            band,
-            band,
-        ],
-        out_specs=(band, band, pl.BlockSpec((part, share), lambda i: (i, 0))),
+        in_specs=[band, band, grad_band],
+        out_specs=(band, band, grad_band),
         compiler_params=pltpu.CompilerParams(vmem_limit_bytes=56 * 2**20),
         name="results",
-    )(attended, dproj, section_out, input_grad)
+    )(section_out, input_grad, weight_grad)
     shape = (1, 1, micro, tok, half)
     return (section_out.reshape(shape), input_grad.reshape(shape), weight_grad[None])
 

time: 111 us -> 101 us (0.910)
  Pallas kernels: 110 us -> 100 us
    pallas_call x1, Pallas kernels: 105 us -> 95.8 us  [per_device(): pl.pallas_call(functools.partial(relay_kernel, (n_dp, n_pipe, n_mp), tile...]
where the time goes in v4:
time: 101 us
  Pallas kernels  100 us (99%)
    pallas_call x1, Pallas kernels, per_device(): pl.pallas_call(functools.partial(relay_kernel, (n_dp, n_pipe, n_mp), tile...  95.8 us
    pallas_call x1, Pallas kernels, per_device(): pl.pallas_call(result_kernel, grid=(tiles,), out_shape=(jax.ShapeDtypeStr...  4.44 us

profile of v4, /device:TPU:0, one launch (start us, length us, event | category | flops | bytes accessed | tf_op | source)
XLA Modules:
  0.0 100.9 jit_solution(10225609044536559252)
XLA Ops:
  0.6 95.8 %relay.1 = (bf16[2,64,1536]{2,1,0:T(8,128)(2,1)}, bf16[2,64,1536]{2,1,0:T(8,128)(2,1)}, f32[768,768]{1,0:T(8,128)}) custom-call(bf16[2,64,3072]{2,1,0:T(8,128)(2,1)} %bitcast.11, bf16[2,128,768]{2,1,0:T(8,128)(2,1)} %bitcast.13, s32[1,128]{1,0:T(1,128)} %mask.1, bf16[4,768,768]{2,1,0:T(8,128)(2,1)} %bitcast.9, bf16[768,3072]{1,0:T(8,128)(2,1)} %bitcast.10, ...), custom_call_target="tpu_custom_call" | custom-call | tf_op jit(solution)/shard_map/relay/pallas_call | solution.py:440
  96.5 4.4 %results.1 = (bf16[2,64,1536]{2,1,0:T(8,128)(2,1)}, bf16[2,64,1536]{2,1,0:T(8,128)(2,1)}, f32[768,768]{1,0:T(8,128)}) custom-call(bf16[2,64,1536]{2,1,0:T(8,128)(2,1)} %get-tuple-element.9.out, bf16[2,64,1536]{2,1,0:T(8,128)(2,1)} %get-tuple-element.10.dx, f32[768,768]{1,0:T(8,128)} %get-tuple-element.11.wg), custom_call_target="tpu_custom_call" | custom-call | tf_op jit(solution)/shard_map/results/pallas_call | solution.py:503

commit v5 on v4

--- a/solution.py
+++ b/solution.py
@@ -10,7 +10,7 @@
 
 HEAD_DIM = 128
 GROUPS = 2
-CHUNKS = 2
+CHUNKS = 3
 MESH = pl.DeviceIdType.MESH
 NT = (((1,), (1,)), ((), ()))
 TN = (((0,), (0,)), ((), ()))
@@ -35,6 +35,7 @@
     wg_ref,
     att_all,
     dcol,
+    att_t,
     wg_vmem,
     wqt,
     wot,
@@ -77,7 +78,9 @@
     inner_width = wo.shape[0]
     heads = inner_width // HEAD_DIM
     share = dpj.shape[2]
-    slabs = chunk // share
+    unit = math.gcd(chunk, share)
+    per_slab = share // unit
+    depth = n_dp * groups * rows
     scale = 1.0 / math.sqrt(HEAD_DIM)
     z = lax.axis_index("dp")
     p = lax.axis_index("pipe")
@@ -266,8 +269,14 @@
 
             relay_copy(dxsend, dybuf, s_dy, r_dy, m, c, h, {"mp": y}, 0).wait_recv()
             dproj = (gate[j] * dybuf[m, h, c].astype(jnp.float32)).astype(jnp.bfloat16)
-            for t in range(slabs):
-                dpj[j * slabs + t, group_rows(m)] = dproj[:, t * share : (t + 1) * share]
+            for t in range(chunk // unit):
+                index = j * (chunk // unit) + t
+                piece = dproj[:, t * unit : (t + 1) * unit]
+                if per_slab == 1:
+                    dpj[index, group_rows(m)] = piece
+                else:
+                    begin = pl.multiple_of(lax.rem(index, per_slab) * unit, unit)
+                    dpj[lax.div(index, per_slab), group_rows(m), pl.ds(begin, unit)] = piece
             d_att += dot(dproj, wot[j])
 
         d_att = d_att.astype(jnp.bfloat16)
@@ -330,23 +339,33 @@
             wqt[j] = wq[j].T
             wot[j] = wo[:, columns(j)].T
 
-    def weight_grad():
-        dcol[z] = dpj[z]
-
+    def turn_attended():
         @pl.loop(0, groups)
         def _(m):
             @pl.loop(1, n_dp)
             def _(k):
-                source = lax.rem(z + n_dp - k, n_dp)
-                att_copy(m, k, source).wait_recv()
-                dproj_copy(m, k, source, z).wait_recv()
-
-        depth = n_dp * groups * rows
+                att_copy(m, k, lax.rem(z + n_dp - k, n_dp)).wait_recv()
+
+        if depth <= 1024:
+            att_t[...] = att_all[...].reshape(depth, inner_width).T
+
+    def weight_grad():
+        dcol[z] = dpj[z]
+
+        @pl.loop(0, groups)
+        def _(m):
+            @pl.loop(1, n_dp)
+            def _(k):
+                dproj_copy(m, k, lax.rem(z + n_dp - k, n_dp), z).wait_recv()
+
         right = dcol[...].reshape(depth, share)
         for i in range(tiles):
             cut = slice(i * (inner_width // tiles), (i + 1) * (inner_width // tiles))
-            left = att_all[:, :, cut].reshape(depth, inner_width // tiles)
-            wg_vmem[cut, :] = dot(left, right, TN)
+            if depth <= 1024:
+                wg_vmem[cut, :] = dot(att_t[cut, :], right)
+            else:
+                left = att_all[:, :, cut].reshape(depth, inner_width // tiles)
+                wg_vmem[cut, :] = dot(left, right, TN)
             keep_grad(i).start()
 
     def keep_grad(i):
@@ -376,6 +395,10 @@
         def _():
             turn_weights()
 
+        @pl.when(step == jnp.where(first, groups, 2 * groups + 2))
+        def _():
+            turn_attended()
+
         phase(backward_query, step - turn)
 
         @pl.when(step == jnp.where(first, 2 * groups, 2 * groups + 2))
@@ -411,10 +434,19 @@
                     backward_copy(m, c, o).wait_send()
 
 
-def result_kernel(out, dx, wg, out_ref, dx_ref, wg_ref):
-    out_ref[...] = out[...]
-    dx_ref[...] = dx[...]
-    wg_ref[...] = wg[...]
+def result_kernel(out, dx, wg, out_ref, dx_ref, wg_ref, sems):
+    parts = sems.shape[0] - 2
+    size = wg.shape[0] // parts
+    copies = [
+        pltpu.make_async_copy(wg.at[pl.ds(i * size, size)], wg_ref.at[pl.ds(i * size, size)], sems.at[i])
+        for i in range(parts)
+    ]
+    copies.append(pltpu.make_async_copy(out, out_ref, sems.at[parts]))
+    copies.append(pltpu.make_async_copy(dx, dx_ref, sems.at[parts + 1]))
+    for copy in copies:
+        copy.start()
+    for copy in copies:
+        copy.wait()
 
 
 def per_device(latents, caption_kv, caption_mask, query_weight, out_weight, gate, cotangent):
@@ -435,7 +467,6 @@
     sem = pltpu.SemaphoreType.DMA
     vmem = pl.BlockSpec(memory_space=pltpu.VMEM)
     tiles = heads // 2 if heads % 2 == 0 and half % (heads // 2 * 128) == 0 else 1
-    part = inner_width // tiles
     anywhere = pl.BlockSpec(memory_space=pl.ANY)
     section_out, input_grad, weight_grad = pl.pallas_call(
         functools.partial(relay_kernel, (n_dp, n_pipe, n_mp), tiles),
@@ -449,6 +480,7 @@
         scratch_shapes=[
             pltpu.VMEM((n_dp, total_rows, inner_width), bf16),
             pltpu.VMEM((n_dp, total_rows, share), bf16),
+            pltpu.VMEM((inner_width, min(n_dp * total_rows, 1024)), bf16),
             pltpu.VMEM((inner_width, share), f32),
             pltpu.VMEM((n_mp * CHUNKS, inner_width, chunk), bf16),
             pltpu.VMEM((n_mp * CHUNKS, chunk, inner_width), bf16),
@@ -498,18 +530,16 @@
         gate.reshape(n_mp * CHUNKS, 1, chunk),
         cotangent.reshape(GROUPS, rows, width),
     )
-    band = pl.BlockSpec((GROUPS, rows, half // tiles), lambda i: (0, 0, i))
-    grad_band = pl.BlockSpec((part, share), lambda i: (i, 0))
     section_out, input_grad, weight_grad = pl.pallas_call(
         result_kernel,
-        grid=(tiles,),
         out_shape=(
             jax.ShapeDtypeStruct((GROUPS, rows, half), bf16),
             jax.ShapeDtypeStruct((GROUPS, rows, half), bf16),
             jax.ShapeDtypeStruct((inner_width, share), f32),
         ),
-        in_specs=[band, band, grad_band],
-        out_specs=(band, band, grad_band),
+        in_specs=[anywhere] * 3,
+        out_specs=(anywhere,) * 3,
+        scratch_shapes=[sem((2 * tiles + 2,))],
         compiler_params=pltpu.CompilerParams(vmem_limit_bytes=56 * 2**20),
         name="results",
     )(section_out, input_grad, weight_grad)

time: 101 us -> 191 us (1.89)
  Pallas kernels: 100 us -> 191 us
    pallas_call x1, Pallas kernels: 4.44 us -> 96.5 us  [per_device(): pl.pallas_call(result_kernel, out_shape=(jax.ShapeDtypeStruct((GROUPS, ro...]
where the time goes in v5:
time: 191 us
  Pallas kernels  191 us (100%)
    pallas_call x1, Pallas kernels, per_device(): pl.pallas_call(result_kernel, out_shape=(jax.ShapeDtypeStruct((GROUPS, ro...  96.5 us
    pallas_call x1, Pallas kernels, per_device(): pl.pallas_call(functools.partial(relay_kernel, (n_dp, n_pipe, n_mp), tile...  94.1 us

profile of v5, /device:TPU:0, one launch (start us, length us, event | category | flops | bytes accessed | tf_op | source)
XLA Modules:
  0.0 191.2 jit_solution(4332376778990474563)
XLA Ops:
  0.6 94.1 %relay.1 = (bf16[2,64,1536]{2,1,0:T(8,128)(2,1)}, bf16[2,64,1536]{2,1,0:T(8,128)(2,1)}, f32[768,768]{1,0:T(8,128)}) custom-call(bf16[2,64,3072]{2,1,0:T(8,128)(2,1)} %bitcast.11, bf16[2,128,768]{2,1,0:T(8,128)(2,1)} %bitcast.13, s32[1,128]{1,0:T(1,128)} %mask.1, bf16[6,512,768]{2,1,0:T(8,128)(2,1)} %bitcast.9, bf16[768,3072]{1,0:T(8,128)(2,1)} %bitcast.10, ...), custom_call_target="tpu_custom_call" | custom-call | tf_op jit(solution)/shard_map/relay/pallas_call | solution.py:471
  94.8 96.5 %results.1 = (bf16[2,64,1536]{2,1,0:T(8,128)(2,1)}, bf16[2,64,1536]{2,1,0:T(8,128)(2,1)}, f32[768,768]{1,0:T(8,128)}) custom-call(bf16[2,64,1536]{2,1,0:T(8,128)(2,1)} %get-tuple-element.9.out, bf16[2,64,1536]{2,1,0:T(8,128)(2,1)} %get-tuple-element.10.dx, f32[768,768]{1,0:T(8,128)} %get-tuple-element.11.wg), custom_call_target="tpu_custom_call" | custom-call | tf_op jit(solution)/shard_map/results/pallas_call | solution.py:533

commit v6 on v5

--- a/solution.py
+++ b/solution.py
@@ -91,9 +91,11 @@
     def load(i, src, dst):
         return pltpu.make_async_copy(src, dst, s_w.at[i])
 
-    load_wq = load(0, wq_any, wq)
-    load_kv = load(1, kv_any, kv)
-    load_wo = load(2, wo_any, wo)
+    def load_wq(j):
+        return load(2 + j, wq_any.at[j], wq.at[j])
+
+    load_kv = load(0, kv_any, kv)
+    load_wo = load(1, wo_any, wo)
 
     def load_rows(src, dst, sems):
         for m in range(groups):
@@ -108,8 +110,10 @@
     def _():
         load_rows(lat, xbuf, r_x)
 
-    load_wq.start()
     load_kv.start()
+    for c in range(chunks):
+        for h in range(n_mp):
+            load_wq(h * chunks + c).start()
     load_wo.start()
 
     @pl.when(last)
@@ -210,7 +214,15 @@
         squares = jnp.zeros((rows, 128), jnp.float32)
         for c, o in order:
             h = lax.rem(y + o, n_mp)
-            relay_copy(xsend, xbuf, s_x, r_x, m, c, h, {"mp": y}, 0).wait_recv()
+            if o == 0:
+                for g in range(n_mp):
+                    relay_copy(xsend, xbuf, s_x, r_x, m, c, g, {"mp": y}, 0).wait_recv()
+
+                @pl.when(jnp.logical_and(first, m == 0))
+                def _():
+                    for g in range(n_mp):
+                        load_wq(g * chunks + c).wait()
+
             x = xbuf[m, h, c]
             query_raw += dot(x, wq[h * chunks + c])
             squares += fold(jnp.square(x.astype(jnp.float32)))
@@ -267,7 +279,10 @@
             h = lax.rem(y + o, n_mp)
             j = h * chunks + c
 
-            relay_copy(dxsend, dybuf, s_dy, r_dy, m, c, h, {"mp": y}, 0).wait_recv()
+            if o == 0:
+                for g in range(n_mp):
+                    relay_copy(dxsend, dybuf, s_dy, r_dy, m, c, g, {"mp": y}, 0).wait_recv()
+
             dproj = (gate[j] * dybuf[m, h, c].astype(jnp.float32)).astype(jnp.bfloat16)
             for t in range(chunk // unit):
                 index = j * (chunk // unit) + t
@@ -372,8 +387,12 @@
         cut = pl.ds(i * (inner_width // tiles), inner_width // tiles)
         return pltpu.make_async_copy(wg_vmem.at[cut], wg_ref.at[cut], s_g.at[i])
 
-    load_wq.wait()
     load_kv.wait()
+
+    @pl.when(jnp.logical_not(first))
+    def _():
+        for j in range(n_mp * chunks):
+            load_wq(j).wait()
 
     @pl.loop(-1, 2 * groups + 3)
     def _(step):
@@ -434,19 +453,27 @@
                     backward_copy(m, c, o).wait_send()
 
 
-def result_kernel(out, dx, wg, out_ref, dx_ref, wg_ref, sems):
-    parts = sems.shape[0] - 2
+def result_kernel(out, dx, wg, out_ref, dx_ref, wg_ref, out_v, dx_v, wg_v, in_sems, out_sems):
+    parts = in_sems.shape[0] - 2
     size = wg.shape[0] // parts
-    copies = [
-        pltpu.make_async_copy(wg.at[pl.ds(i * size, size)], wg_ref.at[pl.ds(i * size, size)], sems.at[i])
-        for i in range(parts)
+    cuts = [pl.ds(i * size, size) for i in range(parts)]
+    routes = [(wg.at[cut], wg_v.at[cut], wg_ref.at[cut]) for cut in cuts]
+    routes += [(out, out_v, out_ref), (dx, dx_v, dx_ref)]
+    loads = [
+        pltpu.make_async_copy(source, held, in_sems.at[i])
+        for i, (source, held, _) in enumerate(routes)
     ]
-    copies.append(pltpu.make_async_copy(out, out_ref, sems.at[parts]))
-    copies.append(pltpu.make_async_copy(dx, dx_ref, sems.at[parts + 1]))
-    for copy in copies:
-        copy.start()
-    for copy in copies:
-        copy.wait()
+    stores = [
+        pltpu.make_async_copy(held, target, out_sems.at[i])
+        for i, (_, held, target) in enumerate(routes)
+    ]
+    for load in loads:
+        load.start()
+    for load, store in zip(loads, stores):
+        load.wait()
+        store.start()
+    for store in stores:
+        store.wait()
 
 
 def per_device(latents, caption_kv, caption_mask, query_weight, out_weight, gate, cotangent):
@@ -502,7 +529,7 @@
             pltpu.VMEM((GROUPS, rows, inner_width), bf16),
             pltpu.VMEM((GROUPS, rows, 128), f32),
             pltpu.VMEM((n_dp, total_rows, share), bf16),
-            sem((3,)),
+            sem((2 + n_mp * CHUNKS,)),
             sem((tiles,)),
             sem((GROUPS, CHUNKS, n_mp)),
             sem((GROUPS, n_mp, CHUNKS)),
@@ -539,7 +566,13 @@
         ),
         in_specs=[anywhere] * 3,
         out_specs=(anywhere,) * 3,
-        scratch_shapes=[sem((2 * tiles + 2,))],
+        scratch_shapes=[
+            pltpu.VMEM((GROUPS, rows, half), bf16),
+            pltpu.VMEM((GROUPS, rows, half), bf16),
+            pltpu.VMEM((inner_width, share), f32),
+            sem((tiles + 2,)),
+            sem((tiles + 2,)),
+        ],
         compiler_params=pltpu.CompilerParams(vmem_limit_bytes=56 * 2**20),
         name="results",
     )(section_out, input_grad, weight_grad)

time: 191 us -> 97.9 us (0.51)
  Pallas kernels: 191 us -> 97 us
    pallas_call x1, Pallas kernels: 96.5 us -> 2.87 us  [per_device(): pl.pallas_call(result_kernel, out_shape=(jax.ShapeDtypeStruct((GROUPS, ro...]
where the time goes in v6:
time: 97.9 us; the launch traced here: 97.6 us
  Pallas kernels  97 us (99%)
    pallas_call x1, Pallas kernels, per_device(): pl.pallas_call(functools.partial(relay_kernel, (n_dp, n_pipe, n_mp), tile...  94.1 us
    pallas_call x1, Pallas kernels, per_device(): pl.pallas_call(result_kernel, out_shape=(jax.ShapeDtypeStruct((GROUPS, ro...  2.87 us

profile of v6, /device:TPU:0, one launch (start us, length us, event | category | flops | bytes accessed | tf_op | source)
XLA Modules:
  0.0 97.6 jit_solution(12029816021766250670)
XLA Ops:
  0.6 94.1 %relay.1 = (bf16[2,64,1536]{2,1,0:T(8,128)(2,1)}, bf16[2,64,1536]{2,1,0:T(8,128)(2,1)}, f32[768,768]{1,0:T(8,128)}) custom-call(bf16[2,64,3072]{2,1,0:T(8,128)(2,1)} %bitcast.11, bf16[2,128,768]{2,1,0:T(8,128)(2,1)} %bitcast.13, s32[1,128]{1,0:T(1,128)} %mask.1, bf16[6,512,768]{2,1,0:T(8,128)(2,1)} %bitcast.9, bf16[768,3072]{1,0:T(8,128)(2,1)} %bitcast.10, ...), custom_call_target="tpu_custom_call" | custom-call | tf_op jit(solution)/shard_map/relay/pallas_call | solution.py:498
  94.7 2.9 %results.1 = (bf16[2,64,1536]{2,1,0:T(8,128)(2,1)}, bf16[2,64,1536]{2,1,0:T(8,128)(2,1)}, f32[768,768]{1,0:T(8,128)}) custom-call(bf16[2,64,1536]{2,1,0:T(8,128)(2,1)} %get-tuple-element.9.out, bf16[2,64,1536]{2,1,0:T(8,128)(2,1)} %get-tuple-element.10.dx, f32[768,768]{1,0:T(8,128)} %get-tuple-element.11.wg), custom_call_target="tpu_custom_call" | custom-call | tf_op jit(solution)/shard_map/results/pallas_call | solution.py:560

commit v7 on v6

--- a/solution.py
+++ b/solution.py
@@ -294,6 +294,10 @@
                     dpj[lax.div(index, per_slab), group_rows(m), pl.ds(begin, unit)] = piece
             d_att += dot(dproj, wot[j])
 
+        @pl.loop(1, n_dp)
+        def _(k):
+            dproj_copy(m, k, z, lax.rem(z + k, n_dp)).start()
+
         d_att = d_att.astype(jnp.bfloat16)
         prob = prob_buf[m]
         d_prob = jnp.stack([dot(d_att[:, head(t)], kv[1, :, head(t)], NT) for t in range(heads)])
@@ -321,10 +325,6 @@
                 share_copy(bsend, brecv, s_b, r_b, m, c, o).start()
         for c in range(chunks):
             own[1, m, c] = piece_of(y, c)
-
-        @pl.loop(1, n_dp)
-        def _(k):
-            dproj_copy(m, k, z, lax.rem(z + k, n_dp)).start()
 
     def backward_finish(m):
         scale_r = rbuf[m][:, :1]

time: 97.9 us -> 95.7 us (0.978)
  Pallas kernels: 97 us -> 94.9 us
    pallas_call x1, Pallas kernels: 94.1 us -> 92 us  [per_device(): pl.pallas_call(functools.partial(relay_kernel, (n_dp, n_pipe, n_mp), tile...]
where the time goes in v7:
time: 95.7 us; the launch traced here: 95.5 us
  Pallas kernels  94.9 us (99%)
    pallas_call x1, Pallas kernels, per_device(): pl.pallas_call(functools.partial(relay_kernel, (n_dp, n_pipe, n_mp), tile...  92 us
    pallas_call x1, Pallas kernels, per_device(): pl.pallas_call(result_kernel, out_shape=(jax.ShapeDtypeStruct((GROUPS, ro...  2.87 us

profile of v7, /device:TPU:0, one launch (start us, length us, event | category | flops | bytes accessed | tf_op | source)
XLA Modules:
  0.0 95.5 jit_solution(4886779168135578762)
XLA Ops:
  0.6 92.0 %relay.1 = (bf16[2,64,1536]{2,1,0:T(8,128)(2,1)}, bf16[2,64,1536]{2,1,0:T(8,128)(2,1)}, f32[768,768]{1,0:T(8,128)}) custom-call(bf16[2,64,3072]{2,1,0:T(8,128)(2,1)} %bitcast.11, bf16[2,128,768]{2,1,0:T(8,128)(2,1)} %bitcast.13, s32[1,128]{1,0:T(1,128)} %mask.1, bf16[6,512,768]{2,1,0:T(8,128)(2,1)} %bitcast.9, bf16[768,3072]{1,0:T(8,128)(2,1)} %bitcast.10, ...), custom_call_target="tpu_custom_call" | custom-call | tf_op jit(solution)/shard_map/relay/pallas_call | solution.py:498
  92.6 2.9 %results.1 = (bf16[2,64,1536]{2,1,0:T(8,128)(2,1)}, bf16[2,64,1536]{2,1,0:T(8,128)(2,1)}, f32[768,768]{1,0:T(8,128)}) custom-call(bf16[2,64,1536]{2,1,0:T(8,128)(2,1)} %get-tuple-element.9.out, bf16[2,64,1536]{2,1,0:T(8,128)(2,1)} %get-tuple-element.10.dx, f32[768,768]{1,0:T(8,128)} %get-tuple-element.11.wg), custom_call_target="tpu_custom_call" | custom-call | tf_op jit(solution)/shard_map/results/pallas_call | solution.py:560
